TPU v7x, 32 devices: a whole 2x2x4 slice. The times are simulated.
32 devices in a mesh: seq: 4 (over x, core), tp: 8 (over z, y).
Axes of the slice: x: 2, y: 2, z: 4, core: 2. Of those that a mesh axis runs over, the one named last changes fastest.
Arguments:
- tokens: bfloat16 [1024, 4096], P('seq', 'tp'), may hold values from -12 to 12
- norm_gain: float32 [2, 4096], replicated, may hold values from 0.5 to 1.5
- w_in: bfloat16 [2, 4096, 2, 8192], P(None, None, None, 'tp'), may hold values from -0.09375 to 0.09375
- w_low: bfloat16 [2, 4096, 288], P(None, 'tp'), may hold values from -0.09375 to 0.09375
- w_dt: bfloat16 [2, 256, 8192], P(None, None, 'tp'), may hold values from -0.75 to 0.75
- a_rate: float32 [2, 16, 8192], P(None, None, 'tp'), may hold values from 0.00048828125 to 0.2
- dt_bias: float32 [2, 8192], P(None, 'tp'), may hold values from -5 to -1
- skip_gain: float32 [2, 8192], P(None, 'tp'), may hold values from 0.5 to 1.5
- threshold: float32 [2, 8192], P(None, 'tp'), may hold values from 0.1 to 0.8
- w_out: bfloat16 [2, 8192, 4096], P(None, 'tp'), may hold values from -0.09375 to 0.09375
Outputs:
- hidden: bfloat16 [1024, 4096], P('seq', 'tp')
All inputs are finite; a program needn't handle non-finite values.
Results may differ from a plain program's by a relative error of at most 0.019.
Values may be sent and summed in bfloat16 or wider, within the bound.
No kernel may reach another device: no remote copies, remote signals or barrier semaphores. Data moves between devices by JAX's collectives and lax.ppermute only.
A program may use at most 192 MiB of HBM per device.

v0:
```python
import functools
import math

import jax
import jax.numpy as jnp
from jax import lax
from jax.experimental import pallas as pl
from jax.experimental.pallas import tpu as pltpu
from jax.sharding import PartitionSpec as P

LANES = 128
WIDE = 256
STRIDE = 3
EPS = 1e-05
DEPTH = 4
LIMIT = 40 * 1024 * 1024
F32 = jnp.float32
BF16 = jnp.bfloat16
VMEM = pl.BlockSpec(memory_space=pltpu.VMEM)
SMEM = pl.BlockSpec(memory_space=pltpu.SMEM)
HBM = pl.BlockSpec(memory_space=pl.ANY)


def row_factor(square_sum, width):
    return lax.rsqrt(square_sum / width + EPS)


def fold_stride(count):
    return STRIDE * count + 1


def params():
    return pltpu.CompilerParams(vmem_limit_bytes=LIMIT)


def proj_kernel(count, first, layer, table_at, depth, table_ref, *refs):
    shards = refs[:count]
    gain_ref, w_ref = refs[count : count + 2]
    cur_ref, gate_ref, square_ref, raw_s, split_s, sems = refs[-6:]
    rows, width = shards[0].shape
    chans = cur_ref.shape[1]
    per = 2 * chans // LANES
    pieces = width // depth
    size = depth * per
    apart = fold_stride(depth)
    begins = [pl.multiple_of(table_ref[table_at + j] * width, width) for j in range(count)]

    def copy(j, q):
        n = j * pieces + q
        return pltpu.make_async_copy(
            w_ref.at[layer, pl.ds(pl.multiple_of((begins[j] + q * depth) * per, size), size), :],
            raw_s.at[n],
            sems.at[n],
        )

    for j in range(count):
        for q in range(pieces):
            copy(j, q).start()
    squares = None if first else square_ref[...]
    for j in range(count):
        values = shards[j][...].astype(F32)
        gain = gain_ref[layer : layer + 1, pl.ds(begins[j], width)]
        scaled = (values * gain).astype(BF16)
        term = jnp.sum(values * values, axis=1, keepdims=True)
        squares = term if squares is None else squares + term
        for q in range(pieces):
            copy(j, q).wait()
            slot = (j * pieces + q) % 2
            raw = raw_s.at[j * pieces + q]

            def spread(n, carried):
                taken = max(per, 16)
                values = raw[pl.ds(pl.multiple_of(n * taken, taken), taken), :].astype(F32)
                for k in range(taken // per):
                    d = n * (taken // per) + k
                    part = values[k * per : (k + 1) * per]
                    split_s[slot, pl.ds(d * STRIDE, per, stride=apart), :] = part
                return carried

            lax.fori_loop(0, size // max(per, 16), spread, 0, unroll=16)
            left = scaled[:, q * depth : (q + 1) * depth]
            for e, out in enumerate((cur_ref, gate_ref)):
                for begin in range(0, chans, WIDE):
                    tiles = [
                        split_s[slot, pl.ds((2 * t + e) * apart, depth, stride=STRIDE), :].astype(BF16)
                        for t in range(begin // LANES, (begin + WIDE) // LANES)
                    ]
                    product = jnp.dot(
                        left, jnp.concatenate(tiles, axis=1), preferred_element_type=F32
                    )
                    cols = slice(begin, begin + WIDE)
                    if first and j == 0 and q == 0:
                        out[:, cols] = product
                    else:
                        out[:, cols] += product
    square_ref[...] = squares


def project(layer, shards, table, table_at, norm_gain, w_raw, chans, before):
    count = len(shards)
    rows, width = shards[0].shape
    depth = min(width, WIDE)
    pieces = count * (width // depth)
    size = depth * 2 * chans // LANES
    state = [jax.ShapeDtypeStruct(s, F32) for s in ((rows, chans), (rows, chans), (rows, 1))]
    operands = [table, *shards, norm_gain, w_raw]
    in_specs = [SMEM] + [VMEM] * (count + 1) + [HBM]
    aliases = {}
    if before is not None:
        aliases = {len(operands) + j: j for j in range(3)}
        in_specs += [VMEM] * 3
        operands += list(before)
    return pl.pallas_call(
        functools.partial(proj_kernel, count, before is None, layer, table_at, depth),
        out_shape=state,
        in_specs=in_specs,
        out_specs=[VMEM] * 3,
        scratch_shapes=[
            pltpu.VMEM((pieces, size, LANES), BF16),
            pltpu.VMEM((2, 2 * chans // LANES * fold_stride(depth), LANES), F32),
            pltpu.SemaphoreType.DMA((pieces,)),
        ],
        input_output_aliases=aliases,
        compiler_params=params(),
        cost_estimate=pl.CostEstimate(
            flops=4 * count * rows * width * chans,
            bytes_accessed=count * (4 * width * chans + 2 * rows * width),
            transcendentals=0,
        ),
        name="project",
    )(*operands)


def scan_kernel(
    layer,
    states,
    width,
    sel_ref,
    low_ref,
    square_ref,
    cur_ref,
    w_dt_ref,
    bias_ref,
    rate_ref,
    out_ref,
    time_ref,
    final_ref,
    step_s,
    drive_s,
):
    rows, chans = cur_ref.shape
    fold = chans // LANES
    rank = w_dt_ref.shape[1]
    factor = row_factor(square_ref[...], width)
    rank_part = (low_ref[:, :rank].astype(F32) * factor).astype(BF16)
    apart = fold_stride(rows)
    twice = factor * factor
    for begin in range(0, chans, WIDE):
        cols = slice(begin, begin + WIDE)
        pre = jnp.dot(rank_part, w_dt_ref[layer, :, cols], preferred_element_type=F32)
        pre = pre + bias_ref[layer : layer + 1, cols]
        step = jnp.maximum(pre, 0.0) + jnp.log1p(jnp.exp(-jnp.abs(pre)))
        drive = step * (cur_ref[:, cols] * twice)
        for q in range(WIDE // LANES):
            part = slice(q * LANES, (q + 1) * LANES)
            place = pl.ds((begin // LANES + q) * apart, rows, stride=STRIDE)
            step_s[place, :] = step[:, part]
            drive_s[place, :] = drive[:, part]

    def advance(t, carried):
        time, held = carried
        here = pl.ds(t * STRIDE, fold, stride=apart)
        step = step_s[here, :]
        drive = drive_s[here, :]
        sums = [None] * 4
        after = []
        for s in range(states):
            decay = jnp.exp2(step * rate_ref[layer, s])
            now = decay * held[s] + drive * sel_ref[t, s]
            term = now * sel_ref[t, states + s]
            sums[s % 4] = term if sums[s % 4] is None else sums[s % 4] + term
            after.append(now)
        time = time + step
        out_ref[here, :] = (sums[0] + sums[1]) + (sums[2] + sums[3])
        time_ref[here, :] = time
        return time, tuple(after)

    zero = jnp.zeros((fold, LANES), F32)
    time, held = lax.fori_loop(0, rows, advance, (zero, (zero,) * states), unroll=4)
    for s in range(states):
        final_ref[s] = held[s].astype(BF16)
    final_ref[states] = time.astype(BF16)


def local_scan(layer, width, selectors, low, square, cur, w_dt, dt_bias, rate):
    rows, chans = cur.shape
    _, states, fold, _ = rate.shape
    folded = (fold * fold_stride(rows), LANES)
    return pl.pallas_call(
        functools.partial(scan_kernel, layer, states, width),
        out_shape=[
            jax.ShapeDtypeStruct(folded, F32),
            jax.ShapeDtypeStruct(folded, F32),
            jax.ShapeDtypeStruct((states + 1, fold, LANES), BF16),
        ],
        in_specs=[SMEM] + [VMEM] * 6,
        out_specs=[VMEM] * 3,
        scratch_shapes=[pltpu.VMEM(folded, F32), pltpu.VMEM(folded, F32)],
        compiler_params=params(),
        cost_estimate=pl.CostEstimate(
            flops=8 * rows * states * chans,
            bytes_accessed=20 * rows * chans,
            transcendentals=rows * states * chans,
        ),
        name="local_scan",
    )(selectors, low, square, cur, w_dt, dt_bias, rate)


def emit_chunks(layer, table_at, feat, gated_ref, table_ref, w_ref, chunks, w_s, sems, before=None):
    def copy(j):
        begin = pl.multiple_of(table_ref[table_at[j]] * feat, feat)
        return pltpu.make_async_copy(w_ref.at[layer, :, pl.ds(begin, feat)], w_s.at[j], sems.at[j])

    for j in range(len(chunks)):
        copy(j).start()
    if before is not None:
        before()
    for j, chunk in enumerate(chunks):
        copy(j).wait()
        for begin in range(0, feat, WIDE):
            cols = slice(begin, begin + WIDE)
            chunk[:, cols] = jnp.dot(
                gated_ref[...], w_s[j, :, cols], preferred_element_type=F32
            ).astype(BF16)


def close_kernel(layer, states, table_at, feat, width, table_ref, place_ref, sel_ref, *refs):
    out_ref, time_ref, cur_ref, gate_ref, square_ref, final_ref = refs[:6]
    rate_ref, skip_ref, thresh_ref, w_ref, gated_ref = refs[6:11]
    chunks = refs[11 : 11 + len(table_at)]
    enter_s, mixed_s, w_s, sems = refs[-4:]
    rows, chans = cur_ref.shape
    fold = chans // LANES
    apart = fold_stride(rows)

    def gate_all():
        def enter(p, state):
            time = final_ref[p, states].astype(F32)
            return tuple(
                jnp.exp2(time * rate_ref[layer, s]) * state[s] + final_ref[p, s].astype(F32)
                for s in range(states)
            )

        zero = jnp.zeros((fold, LANES), F32)
        state = lax.fori_loop(0, place_ref[0], enter, (zero,) * states)
        for s in range(states):
            enter_s[s] = state[s]

        def correct(t, carried):
            here = pl.ds(t * STRIDE, fold, stride=apart)
            time = time_ref[here, :]
            sums = [out_ref[here, :], None, None, None]
            for s in range(states):
                term = jnp.exp2(time * rate_ref[layer, s]) * (enter_s[s] * sel_ref[t, states + s])
                sums[s % 4] = term if sums[s % 4] is None else sums[s % 4] + term
            mixed_s[here, :] = (sums[0] + sums[1]) + (sums[2] + sums[3])
            return carried

        lax.fori_loop(0, rows, correct, 0, unroll=4)

        factor = row_factor(square_ref[...], width)
        for r in range(fold):
            cols = slice(r * LANES, (r + 1) * LANES)
            skip = skip_ref[layer : layer + 1, cols]
            mixed = mixed_s[pl.ds(r * apart, rows, stride=STRIDE), :] + skip * cur_ref[:, cols]
            mixed = mixed * factor
            normal = mixed * lax.rsqrt(jnp.mean(mixed * mixed, axis=1, keepdims=True) + EPS)
            thresh = thresh_ref[layer : layer + 1, cols]
            shrunk = jnp.maximum(normal - thresh, 0.0) - jnp.maximum(-normal - thresh, 0.0)
            gate = gate_ref[:, cols] * factor
            gated_ref[:, cols] = (shrunk * (gate * jax.nn.sigmoid(gate))).astype(BF16)

    emit_chunks(layer, table_at, feat, gated_ref, table_ref, w_ref, chunks, w_s, sems, gate_all)


def close_layer(
    layer, width, table, table_at, feat, seq_place, selectors, values, rate, skip, thresh, w_out
):
    rows, chans = values[2].shape
    _, states, fold, _ = rate.shape
    count = len(table_at)
    chunk = jax.ShapeDtypeStruct((rows, feat), BF16)
    results = pl.pallas_call(
        functools.partial(close_kernel, layer, states, table_at, feat, width),
        out_shape=[jax.ShapeDtypeStruct((rows, chans), BF16)] + [chunk] * count,
        in_specs=[SMEM] * 3 + [VMEM] * 9 + [HBM],
        out_specs=[VMEM] * (1 + count),
        scratch_shapes=[
            pltpu.VMEM((states, fold, LANES), F32),
            pltpu.VMEM((fold * fold_stride(rows), LANES), F32),
            pltpu.VMEM((count, chans, feat), BF16),
            pltpu.SemaphoreType.DMA((count,)),
        ],
        compiler_params=params(),
        cost_estimate=pl.CostEstimate(
            flops=6 * rows * states * chans + 2 * count * rows * chans * feat,
            bytes_accessed=20 * rows * chans + 2 * count * chans * feat,
            transcendentals=rows * states * chans,
        ),
        name="close_layer",
    )(table, seq_place, selectors, *values, rate, skip, thresh, w_out)
    return results[0], results[1:]


def expand_kernel(layer, table_at, feat, table_ref, gated_ref, w_ref, *refs):
    chunks = refs[: len(table_at)]
    emit_chunks(layer, table_at, feat, gated_ref, table_ref, w_ref, chunks, *refs[-2:])


def expand(layer, table, table_at, feat, gated, w_out):
    rows, chans = gated.shape
    count = len(table_at)
    return pl.pallas_call(
        functools.partial(expand_kernel, layer, table_at, feat),
        out_shape=[jax.ShapeDtypeStruct((rows, feat), BF16)] * count,
        in_specs=[SMEM, VMEM, HBM],
        out_specs=[VMEM] * count,
        scratch_shapes=[
            pltpu.VMEM((count, chans, feat), BF16),
            pltpu.SemaphoreType.DMA((count,)),
        ],
        compiler_params=params(),
        cost_estimate=pl.CostEstimate(
            flops=2 * count * rows * chans * feat,
            bytes_accessed=2 * count * chans * feat + 2 * (count + 2) * rows * feat,
            transcendentals=0,
        ),
        name="expand",
    )(table, gated, w_out)


class Grid:
    def __init__(self, count):
        self.depth = DEPTH if count % DEPTH == 0 else 1
        self.side = count // self.depth

    def places(self):
        return [(z, y) for z in range(self.depth) for y in range(self.side)]

    def at(self, z, y):
        return (z % self.depth) * self.side + y % self.side

    def send(self, value, deep, across):
        pairs = [(self.at(z, y), self.at(z + deep, y + across)) for z, y in self.places()]
        return lax.ppermute(value, "tp", pairs)

    def swap(self, value, bit):
        pairs = [(self.at(z, y), self.at(z ^ bit, y)) for z, y in self.places()]
        return lax.ppermute(value, "tp", pairs)

    def table(self):
        own = lax.axis_index("tp")
        z, y = own // self.side, own % self.side
        offsets = jnp.arange(self.depth * self.side, dtype=jnp.int32)
        a, b = offsets // self.side, offsets % self.side
        both = []
        for sign in (-1, 1):
            deep = (z + sign * a + self.depth) % self.depth
            both.append(deep * self.side + (y + sign * b + self.side) % self.side)
        return jnp.concatenate(both).astype(jnp.int32)


def after(value, *others):
    return lax.optimization_barrier((value, others))[0]


def gather_columns(grid, own):
    columns = {0: own}
    half = grid.depth // 2
    for a in range(1, grid.depth - half + 1):
        columns[a] = grid.send(columns[a - 1], 1, 0)
        back = grid.depth - a
        if back > a:
            columns[back] = grid.send(columns[(back + 1) % grid.depth], -1, 0)
    return columns


def scatter_order(grid):
    order = []
    for a in range(grid.depth - grid.depth // 2, 0, -1):
        if grid.depth - a > a:
            order.append(grid.depth - a)
        order.append(a)
    return order + [0]


def scatter_sum(grid, own_rows, chunks):
    crossed = {
        (a, b): grid.send(chunks[a, b], 0, b)
        for a in scatter_order(grid)
        for b in range(1, grid.side)
    }
    half = grid.depth - grid.depth // 2
    arriving = {}
    for a in scatter_order(grid):
        part = chunks[a, 0].astype(F32)
        for b in range(1, grid.side):
            part = part + crossed[a, b].astype(F32)
        if a == 0:
            total = own_rows.astype(F32) + part
        elif a <= half:
            if a in arriving:
                part = part + arriving[a].astype(F32)
            arriving[a - 1] = grid.send(part.astype(BF16), 1, 0)
        else:
            if a in arriving:
                part = part + arriving[a].astype(F32)
            after = (a + 1) % grid.depth
            moved = grid.send(part.astype(BF16), -1, 0)
            if after == 0:
                last = moved
            else:
                arriving[after] = moved
    if grid.depth > 1:
        total = total + arriving[0].astype(F32)
    if grid.depth > 2:
        total = total + last.astype(F32)
    return total.astype(BF16)


def sum_selectors(grid, partial, arrivals):
    arrivals = list(arrivals)
    rows = partial.shape[0]
    part = rows // grid.side
    own_y = lax.axis_index("tp") % grid.side
    piece = lambda y: lax.dynamic_slice_in_dim(partial, (y % grid.side) * part, part, 0)
    total = piece(own_y).astype(F32)
    for b in range(1, grid.side):
        total = total + grid.send(piece(own_y + b), 0, b).astype(F32)
    bit = 1
    while bit < grid.depth:
        total = after(total.astype(BF16), arrivals.pop(0))
        total = total.astype(F32) + grid.swap(total, bit).astype(F32)
        bit *= 2
    total = after(total.astype(BF16), arrivals.pop(0))
    result = jnp.zeros_like(partial)
    for b in range(grid.side):
        got = grid.send(total, 0, b) if b else total
        place = ((own_y - b + grid.side) % grid.side) * part
        result = lax.dynamic_update_slice_in_dim(result, got, place, 0)
    return result


def per_device(
    n_tp, tokens, norm_gain, w_in, w_low, w_dt, a_rate, dt_bias, skip_gain, threshold, w_out
):
    grid = Grid(n_tp)
    feat = tokens.shape[1]
    layers, width, _, chans = w_in.shape
    states = a_rate.shape[1]
    rank = w_dt.shape[1]
    fold = chans // LANES
    table = grid.table()
    forth = lambda a, b: n_tp + a * grid.side + b
    seq_place = lax.axis_index("seq").astype(jnp.int32).reshape(1)
    own_place = lax.axis_index("tp") * feat
    rates = (a_rate * (-math.log2(math.e))).reshape(layers, states, fold, LANES)
    w_raw = w_in.reshape(layers, width, 2, fold, LANES).transpose(0, 1, 3, 2, 4)
    w_raw = w_raw.reshape(layers, width * 2 * fold, LANES)
    own_gain = lax.dynamic_slice_in_dim(norm_gain, own_place, feat, 1)
    order = scatter_order(grid)
    own_rows = tokens
    for layer in range(layers):
        columns = gather_columns(grid, own_rows)
        arrivals = order[::-1]
        scaled = (own_rows.astype(F32) * own_gain[layer]).astype(BF16)
        low = jnp.dot(scaled, w_low[layer], preferred_element_type=F32).astype(BF16)
        low = sum_selectors(grid, low, [columns[a] for a in arrivals[1:]])
        selectors = low[:, rank:].astype(F32)
        state = None
        squares = []
        for n, a in enumerate(arrivals):
            column = after(columns[a], squares[n - 2]) if n > 1 else columns[a]
            arrived = [column] + [grid.send(column, 0, b) for b in range(1, grid.side)]
            state = project(
                layer, arrived, table, a * grid.side, norm_gain, w_raw, chans, state
            )
            squares.append(state[2])
        cur, gate, square = state
        out, time, final = local_scan(
            layer, width, selectors, low, square, cur, w_dt, dt_bias, rates
        )
        finals = lax.all_gather(final, "seq")
        keys = [(a, b) for a in order for b in range(1, grid.side)]
        keys += [(a, 0) for a in order]
        lead = grid.side - 1
        gated, chunks = close_layer(
            layer,
            width,
            table,
            [forth(*key) for key in keys[:lead]],
            feat,
            seq_place,
            selectors,
            (out, time, cur, gate, square, finals),
            rates,
            skip_gain,
            threshold,
            w_out,
        )
        others = expand(layer, table, [forth(*key) for key in keys[lead:]], feat, gated, w_out)
        own_rows = scatter_sum(grid, own_rows, dict(zip(keys, [*chunks, *others])))
    return own_rows


def solution(mesh):
    in_specs = (
        P("seq", "tp"),
        P(),
        P(None, None, None, "tp"),
        P(None, "tp", None),
        P(None, None, "tp"),
        P(None, None, "tp"),
        P(None, "tp"),
        P(None, "tp"),
        P(None, "tp"),
        P(None, "tp", None),
    )
    return jax.shard_map(
        functools.partial(per_device, mesh.shape["tp"]),
        mesh=mesh,
        in_specs=in_specs,
        out_specs=P("seq", "tp"),
        check_vma=False,
    )
```

profile of v0, /device:TPU:0, one launch (start us, length us, event | category | flops | bytes accessed | tf_op | source)
XLA Modules:
  0.0 204.6 jit_solution(6366277650470415961)
XLA Ops:
  0.0 5.0 %collective-permute-start.3 = (bf16[256,512]{1,0:T(8,128)(2,1)}, bf16[256,512]{1,0:T(8,128)(2,1)S(1)}, u32[]{:S(2)}, u32[]{:S(2)}) collective-permute-start(bf16[256,512]{1,0:T(8,128)(2,1)} %refs_0_.1), channel_id=1, source_target_pairs={{0,6},{1,7},{2,0},{3,1},{4,2},{5,3},{6,4},{7,5},{8,14},{9,15},{10,... | collective-permute-start | bytes 786440 | tf_op jit(solution)/shard_map/ppermute | solution.py:355
  10.3 4.8 %collective-permute-done = bf16[128,288]{1,0:T(8,128)(2,1)S(1)} collective-permute-done((bf16[128,288]{1,0:T(8,128)(2,1)S(1)}, bf16[128,288]{1,0:T(8,128)(2,1)S(1)}, u32[]{:S(2)}, u32[]{:S(2)}) %collective-permute-start) | collective-permute-done | bytes 73760 | tf_op jit(solution)/shard_map/ppermute | solution.py:355
  24.6 4.6 %project.8 = (f32[256,1024]{1,0:T(8,128)S(1)}, f32[256,1024]{1,0:T(8,128)S(1)}, f32[256,1]{1,0:T(8,128)S(1)}) custom-call(s32[16]{0:T(128)S(1)} %pad_add_fusion.table_ref, bf16[256,512]{1,0:T(8,128)(2,1)S(1)} %copy-done.2, bf16[256,512]{1,0:T(8,128)(2,1)S(1)} %collective-permute-done.8.refs_1_, f32[2,4096]{1,0:T(2,128)S(1)} %copy-done, ...), custom_call_target="tpu_custom_call" | custom-call | flops 1073741824 | bytes 4718592 | tf_op jit(solution)/shard_map/project/pallas_call | solution.py:113
  30.9 2.3 %collective-permute-done.4 = bf16[128,288]{1,0:T(8,128)(2,1)S(1)} collective-permute-done((bf16[128,288]{1,0:T(8,128)(2,1)S(1)}, bf16[128,288]{1,0:T(8,128)(2,1)S(1)}, u32[]{:S(2)}, u32[]{:S(2)}) %collective-permute-start.4) | collective-permute-done | bytes 73760 | tf_op jit(solution)/shard_map/ppermute | solution.py:359
  34.0 4.6 %project.9 = (f32[256,1024]{1,0:T(8,128)S(1)}, f32[256,1024]{1,0:T(8,128)S(1)}, f32[256,1]{1,0:T(8,128)S(1)}) custom-call(s32[16]{0:T(128)S(1)} %pad_add_fusion.table_ref, bf16[256,512]{1,0:T(8,128)(2,1)S(1)} %collective-permute-done.1.refs_0_, ...), custom_call_target="tpu_custom_call", output_to_operand_aliasing={{0}: (5, {}), {1}: (6, {}), {2}: (7, {})} | custom-call | flops 1073741824 | bytes 4718592 | tf_op jit(solution)/shard_map/project/pallas_call | solution.py:113
  40.1 4.6 %project.10 = (f32[256,1024]{1,0:T(8,128)S(1)}, f32[256,1024]{1,0:T(8,128)S(1)}, f32[256,1]{1,0:T(8,128)S(1)}) custom-call(s32[16]{0:T(128)S(1)} %pad_add_fusion.table_ref, bf16[256,512]{1,0:T(8,128)(2,1)S(1)} %collective-permute-done.3.refs_0_, ...), custom_call_target="tpu_custom_call", output_to_operand_aliasing={{0}: (5, {}), {1}: (6, {}), {2}: (7, {})} | custom-call | flops 1073741824 | bytes 4718592 | tf_op jit(solution)/shard_map/project/pallas_call | solution.py:113
  46.6 4.6 %project.11 = (f32[256,1024]{1,0:T(8,128)S(1)}, f32[256,1024]{1,0:T(8,128)S(1)}, f32[256,1]{1,0:T(8,128)S(1)}) custom-call(s32[16]{0:T(128)S(1)} %pad_add_fusion.table_ref, bf16[256,512]{1,0:T(8,128)(2,1)S(1)} %collective-permute-done.5.refs_0_, ...), custom_call_target="tpu_custom_call", output_to_operand_aliasing={{0}: (5, {}), {1}: (6, {}), {2}: (7, {})} | custom-call | flops 1073741824 | bytes 4718592 | tf_op jit(solution)/shard_map/project/pallas_call | solution.py:113
  51.3 9.1 %local_scan.2 = (f32[6152,128]{1,0:T(8,128)S(1)}, f32[6152,128]{1,0:T(8,128)S(1)}, bf16[17,8,128]{2,1,0:T(8,128)(2,1)S(1)}) custom-call(f32[256,32]{1,0:T(8,128)S(1)} %slice_convert_fusion.1.sel_ref, bf16[256,288]{1,0:T(8,128)(2,1)S(1)} %constant_dynamic-update-slice_fusion.2.low_ref, f32[256,1]{1,0:T(8,128)S(1)} %get-tuple-element.77.square_ref.refs_4_, ...), custom_call_target="tpu_custom_call" | custom-call | flops 33554432 | bytes 5242880 | tf_op jit(solution)/shard_map/local_scan/pallas_call | solution.py:199
  60.4 5.4 %all-gather = bf16[68,8,128]{2,1,0:T(8,128)(2,1)S(1)} all-gather(bf16[17,8,128]{2,1,0:T(8,128)(2,1)S(1)} %get-tuple-element.82), channel_id=2, replica_groups=mesh['seq'=4,'tp'=8] {'seq'}, dimensions={0}, use_global_device_ids=true | all-gather | bytes 174080 | tf_op jit(solution)/shard_map/all_gather | solution.py:493
  65.9 7.8 %close_layer.2 = (bf16[256,1024]{1,0:T(8,128)(2,1)S(1)}, bf16[256,512]{1,0:T(8,128)(2,1)S(1)}) custom-call(s32[16]{0:T(128)S(1)} %pad_add_fusion.table_ref, s32[1]{0:T(128)} %bitcast.place_ref, f32[256,32]{1,0:T(8,128)S(1)} %slice_convert_fusion.1.sel_ref, f32[6152,128]{1,0:T(8,128)S(1)} %get-tuple-element.79.refs_0_, ...), custom_call_target="tpu_custom_call" | custom-call | flops 293601280 | bytes 6291456 | tf_op jit(solution)/shard_map/close_layer/pallas_call | solution.py:293
  75.0 4.9 %expand.2 = (bf16[256,512]{1,0:T(8,128)(2,1)S(1)}, bf16[256,512]{1,0:T(8,128)(2,1)S(1)}, bf16[256,512]{1,0:T(8,128)(2,1)S(1)}, bf16[256,512]{1,0:T(8,128)(2,1)S(...) custom-call(s32[16]{0:T(128)S(1)} %pad_add_fusion.table_ref, ...), custom_call_target="tpu_custom_call" | custom-call | flops 1879048192 | bytes 9699328 | tf_op jit(solution)/shard_map/expand/pallas_call | solution.py:323
  83.8 5.3 %collective-permute-done.16 = bf16[256,512]{1,0:T(8,128)(2,1)S(1)} collective-permute-done((bf16[256,512]{1,0:T(8,128)(2,1)S(1)}, bf16[256,512]{1,0:T(8,128)(2,1)S(1)}, u32[]{:S(2)}, u32[]{:S(2)}) %collective-permute-start.16) | collective-permute-done | bytes 262176 | tf_op jit(solution)/shard_map/ppermute | solution.py:355
  89.7 5.0 %collective-permute-done.12 = bf16[256,512]{1,0:T(8,128)(2,1)S(1)} collective-permute-done((bf16[256,512]{1,0:T(8,128)(2,1)S(1)}, bf16[256,512]{1,0:T(8,128)(2,1)S(1)}, u32[]{:S(2)}, u32[]{:S(2)}) %collective-permute-start.12) | collective-permute-done | bytes 262176 | tf_op jit(solution)/shard_map/ppermute | solution.py:355
  95.1 4.4 %collective-permute-done.11 = bf16[256,512]{1,0:T(8,128)(2,1)S(1)} collective-permute-done((bf16[256,512]{1,0:T(8,128)(2,1)S(1)}, bf16[256,512]{1,0:T(8,128)(2,1)S(1)}, u32[]{:S(2)}, u32[]{:S(2)}) %collective-permute-start.11) | collective-permute-done | bytes 262176 | tf_op jit(solution)/shard_map/ppermute | solution.py:355
  99.5 4.0 %collective-permute-done.15 = bf16[256,512]{1,0:T(8,128)(2,1)S(1)} collective-permute-done((bf16[256,512]{1,0:T(8,128)(2,1)S(1)}, bf16[256,512]{1,0:T(8,128)(2,1)S(1)}, u32[]{:S(2)}, u32[]{:S(2)}) %collective-permute-start.15) | collective-permute-done | bytes 262176 | tf_op jit(solution)/shard_map/ppermute | solution.py:355
  105.2 3.5 %collective-permute-done.18 = bf16[128,288]{1,0:T(8,128)(2,1)S(1)} collective-permute-done((bf16[128,288]{1,0:T(8,128)(2,1)S(1)}, bf16[128,288]{1,0:T(8,128)(2,1)S(1)}, u32[]{:S(2)}, u32[]{:S(2)}) %collective-permute-start.18) | collective-permute-done | bytes 73760 | tf_op jit(solution)/shard_map/ppermute | solution.py:355
  108.7 4.7 %collective-permute-done.19.refs_0_ = bf16[256,512]{1,0:T(8,128)(2,1)S(1)} collective-permute-done((bf16[256,512]{1,0:T(8,128)(2,1)S(1)}, bf16[256,512]{1,0:T(8,128)(2,1)S(1)}, u32[]{:S(2)}, u32[]{:S(2)}) %collective-permute-start.19) | collective-permute-done | bytes 262176 | tf_op jit(solution)/shard_map/ppermute | solution.py:355
  118.3 7.3 %collective-permute-done.21.refs_0_ = bf16[256,512]{1,0:T(8,128)(2,1)S(1)} collective-permute-done((bf16[256,512]{1,0:T(8,128)(2,1)S(1)}, bf16[256,512]{1,0:T(8,128)(2,1)S(1)}, u32[]{:S(2)}, u32[]{:S(2)}) %collective-permute-start.21) | collective-permute-done | bytes 262176 | tf_op jit(solution)/shard_map/ppermute | solution.py:355
  125.6 2.5 %collective-permute-start.22 = (bf16[128,288]{1,0:T(8,128)(2,1)S(1)}, bf16[128,288]{1,0:T(8,128)(2,1)S(1)}, u32[]{:S(2)}, u32[]{:S(2)}) collective-permute-start(bf16[128,288]{1,0:T(8,128)(2,1)S(1)} %add_convert_fusion.7), channel_id=1, source_target_pairs={{0,4},{1,5},{2,6},{3,7},{4,0},{5,1},{6,2},{7,3},{8,12},{9,13},{10,... | collective-permute-start | bytes 221192 | tf_op jit(solution)/shard_map/ppermute | solution.py:359
  128.1 4.6 %project.12 = (f32[256,1024]{1,0:T(8,128)S(1)}, f32[256,1024]{1,0:T(8,128)S(1)}, f32[256,1]{1,0:T(8,128)S(1)}) custom-call(s32[16]{0:T(128)S(1)} %pad_add_fusion.table_ref, bf16[256,512]{1,0:T(8,128)(2,1)S(1)} %fusion.3.refs_0_, bf16[256,512]{1,0:T(8,128)(2,1)S(1)} %collective-permute-done.26.refs_1_, f32[2,4096]{1,0:T(2,128)S(1)} %copy-done.1, ...), custom_call_target="tpu_custom_call" | custom-call | flops 1073741824 | bytes 4718592 | tf_op jit(solution)/shard_map/project/pallas_call | solution.py:113
  135.0 4.6 %project.13 = (f32[256,1024]{1,0:T(8,128)S(1)}, f32[256,1024]{1,0:T(8,128)S(1)}, f32[256,1]{1,0:T(8,128)S(1)}) custom-call(s32[16]{0:T(128)S(1)} %pad_add_fusion.table_ref, bf16[256,512]{1,0:T(8,128)(2,1)S(1)} %collective-permute-done.19.refs_0_, ...), custom_call_target="tpu_custom_call", output_to_operand_aliasing={{0}: (5, {}), {1}: (6, {}), {2}: (7, {})} | custom-call | flops 1073741824 | bytes 4718592 | tf_op jit(solution)/shard_map/project/pallas_call | solution.py:113
  142.0 4.6 %project.14 = (f32[256,1024]{1,0:T(8,128)S(1)}, f32[256,1024]{1,0:T(8,128)S(1)}, f32[256,1]{1,0:T(8,128)S(1)}) custom-call(s32[16]{0:T(128)S(1)} %pad_add_fusion.table_ref, bf16[256,512]{1,0:T(8,128)(2,1)S(1)} %collective-permute-done.21.refs_0_, ...), custom_call_target="tpu_custom_call", output_to_operand_aliasing={{0}: (5, {}), {1}: (6, {}), {2}: (7, {})} | custom-call | flops 1073741824 | bytes 4718592 | tf_op jit(solution)/shard_map/project/pallas_call | solution.py:113
  146.7 4.6 %project.15 = (f32[256,1024]{1,0:T(8,128)S(1)}, f32[256,1024]{1,0:T(8,128)S(1)}, f32[256,1]{1,0:T(8,128)S(1)}) custom-call(s32[16]{0:T(128)S(1)} %pad_add_fusion.table_ref, bf16[256,512]{1,0:T(8,128)(2,1)S(1)} %collective-permute-done.23.refs_0_, ...), custom_call_target="tpu_custom_call", output_to_operand_aliasing={{0}: (5, {}), {1}: (6, {}), {2}: (7, {})} | custom-call | flops 1073741824 | bytes 4718592 | tf_op jit(solution)/shard_map/project/pallas_call | solution.py:113
  151.4 9.1 %local_scan.3 = (f32[6152,128]{1,0:T(8,128)S(1)}, f32[6152,128]{1,0:T(8,128)S(1)}, bf16[17,8,128]{2,1,0:T(8,128)(2,1)S(1)}) custom-call(f32[256,32]{1,0:T(8,128)S(1)} %slice_convert_fusion.sel_ref, bf16[256,288]{1,0:T(8,128)(2,1)S(1)} %constant_dynamic-update-slice_fusion.low_ref, f32[256,1]{1,0:T(8,128)S(1)} %get-tuple-element.106.square_ref.refs_4_, ...), custom_call_target="tpu_custom_call" | custom-call | flops 33554432 | bytes 5242880 | tf_op jit(solution)/shard_map/local_scan/pallas_call | solution.py:199
  160.5 5.4 %all-gather.1 = bf16[68,8,128]{2,1,0:T(8,128)(2,1)S(1)} all-gather(bf16[17,8,128]{2,1,0:T(8,128)(2,1)S(1)} %get-tuple-element.111), channel_id=3, replica_groups=mesh['seq'=4,'tp'=8] {'seq'}, dimensions={0}, use_global_device_ids=true | all-gather | bytes 174080 | tf_op jit(solution)/shard_map/all_gather | solution.py:493
  165.9 7.8 %close_layer.3 = (bf16[256,1024]{1,0:T(8,128)(2,1)S(1)}, bf16[256,512]{1,0:T(8,128)(2,1)S(1)}) custom-call(s32[16]{0:T(128)S(1)} %pad_add_fusion.table_ref, s32[1]{0:T(128)} %bitcast.place_ref, f32[256,32]{1,0:T(8,128)S(1)} %slice_convert_fusion.sel_ref, f32[6152,128]{1,0:T(8,128)S(1)} %get-tuple-element.108.refs_0_, ...), custom_call_target="tpu_custom_call" | custom-call | flops 293601280 | bytes 6291456 | tf_op jit(solution)/shard_map/close_layer/pallas_call | solution.py:293
  175.4 4.9 %expand.3 = (bf16[256,512]{1,0:T(8,128)(2,1)S(1)}, bf16[256,512]{1,0:T(8,128)(2,1)S(1)}, bf16[256,512]{1,0:T(8,128)(2,1)S(1)}, bf16[256,512]{1,0:T(8,128)(2,1)S(...) custom-call(s32[16]{0:T(128)S(1)} %pad_add_fusion.table_ref, ...), custom_call_target="tpu_custom_call" | custom-call | flops 1879048192 | bytes 9699328 | tf_op jit(solution)/shard_map/expand/pallas_call | solution.py:323
  184.9 4.7 %collective-permute-done.34 = bf16[256,512]{1,0:T(8,128)(2,1)S(1)} collective-permute-done((bf16[256,512]{1,0:T(8,128)(2,1)S(1)}, bf16[256,512]{1,0:T(8,128)(2,1)S(1)}, u32[]{:S(2)}, u32[]{:S(2)}) %collective-permute-start.34) | collective-permute-done | bytes 262176 | tf_op jit(solution)/shard_map/ppermute | solution.py:355
  189.7 3.2 %collective-permute-start.35 = (bf16[256,512]{1,0:T(8,128)(2,1)S(1)}, bf16[256,512]{1,0:T(8,128)(2,1)S(1)}, u32[]{:S(2)}, u32[]{:S(2)}) collective-permute-start(bf16[256,512]{1,0:T(8,128)(2,1)S(1)} %add_convert_fusion), channel_id=1, source_target_pairs={{0,6},{1,7},{2,0},{3,1},{4,2},{5,3},{6,4},{7,5},{8,14},{9,15},{10,... | collective-permute-start | bytes 786440 | tf_op jit(solution)/shard_map/ppermute | solution.py:355
  192.8 2.4 %collective-permute-done.30 = bf16[256,512]{1,0:T(8,128)(2,1)S(1)} collective-permute-done((bf16[256,512]{1,0:T(8,128)(2,1)S(1)}, bf16[256,512]{1,0:T(8,128)(2,1)S(1)}, u32[]{:S(2)}, u32[]{:S(2)}) %collective-permute-start.30) | collective-permute-done | bytes 262176 | tf_op jit(solution)/shard_map/ppermute | solution.py:355
  196.1 3.8 %collective-permute-done.29 = bf16[256,512]{1,0:T(8,128)(2,1)S(1)} collective-permute-done((bf16[256,512]{1,0:T(8,128)(2,1)S(1)}, bf16[256,512]{1,0:T(8,128)(2,1)S(1)}, u32[]{:S(2)}, u32[]{:S(2)}) %collective-permute-start.29) | collective-permute-done | bytes 262176 | tf_op jit(solution)/shard_map/ppermute | solution.py:355
  200.0 3.8 %collective-permute-done.33 = bf16[256,512]{1,0:T(8,128)(2,1)S(1)} collective-permute-done((bf16[256,512]{1,0:T(8,128)(2,1)S(1)}, bf16[256,512]{1,0:T(8,128)(2,1)S(1)}, u32[]{:S(2)}, u32[]{:S(2)}) %collective-permute-start.33) | collective-permute-done | bytes 262176 | tf_op jit(solution)/shard_map/ppermute | solution.py:355
  (105 shorter events, 45.9 us)
Async XLA Ops:
  0.0 22.1 %collective-permute-start.3 = (bf16[256,512]{1,0:T(8,128)(2,1)}, bf16[256,512]{1,0:T(8,128)(2,1)S(1)}, u32[]{:S(2)}, u32[]{:S(2)}) collective-permute-start(bf16[256,512]{1,0:T(8,128)(2,1)} %refs_0_.1), channel_id=1, source_target_pairs={{0,6},{1,7},{2,0},{3,1},{4,2},{5,3},{6,4},{7,5},{8,14},{9,15},{10,... | collective-permute-start | bytes 786440 | tf_op jit(solution)/shard_map/ppermute | solution.py:355
  5.0 12.3 %collective-permute-start.1 = (bf16[256,512]{1,0:T(8,128)(2,1)}, bf16[256,512]{1,0:T(8,128)(2,1)S(1)}, u32[]{:S(2)}, u32[]{:S(2)}) collective-permute-start(bf16[256,512]{1,0:T(8,128)(2,1)} %refs_0_.1), channel_id=1, source_target_pairs={{0,2},{1,3},{2,4},{3,5},{4,6},{5,7},{6,0},{7,1},{8,10},{9,11},{10,... | collective-permute-start | bytes 786440 | tf_op jit(solution)/shard_map/ppermute | solution.py:355
  5.1 17.9 %collective-permute-start.8 = (bf16[256,512]{1,0:T(8,128)(2,1)}, bf16[256,512]{1,0:T(8,128)(2,1)S(1)}, u32[]{:S(2)}, u32[]{:S(2)}) collective-permute-start(bf16[256,512]{1,0:T(8,128)(2,1)} %refs_0_.1), channel_id=1, source_target_pairs={{0,1},{1,0},{2,3},{3,2},{4,5},{5,4},{6,7},{7,6},{8,9},{9,8},{10,11... | collective-permute-start | bytes 786440 | tf_op jit(solution)/shard_map/ppermute | solution.py:355
  19.1 14.9 %collective-permute-start.7 = (bf16[256,512]{1,0:T(8,128)(2,1)S(1)}, bf16[256,512]{1,0:T(8,128)(2,1)S(1)}, u32[]{:S(2)}, u32[]{:S(2)}) collective-permute-start(bf16[256,512]{1,0:T(8,128)(2,1)S(1)} %collective-permute-done.1.refs_0_), channel_id=1, source_target_pairs={{0,1},{1,0},{2,3},{3,2},{4,5},{5,4},{6,7},{7,6},{8,9},{9,8},{10,11... | collective-permute-start | bytes 786440 | tf_op jit(solution)/shard_map/ppermute | solution.py:355
  20.7 12.6 %collective-permute-start.5 = (bf16[256,512]{1,0:T(8,128)(2,1)S(1)}, bf16[256,512]{1,0:T(8,128)(2,1)S(1)}, u32[]{:S(2)}, u32[]{:S(2)}) collective-permute-start(bf16[256,512]{1,0:T(8,128)(2,1)S(1)} %collective-permute-done.1.refs_0_), channel_id=1, source_target_pairs={{0,2},{1,3},{2,4},{3,5},{4,6},{5,7},{6,0},{7,1},{8,10},{9,11},{10,... | collective-permute-start | bytes 786440 | tf_op jit(solution)/shard_map/ppermute | solution.py:355
  22.1 11.1 %collective-permute-start.4 = (bf16[128,288]{1,0:T(8,128)(2,1)S(1)}, bf16[128,288]{1,0:T(8,128)(2,1)S(1)}, u32[]{:S(2)}, u32[]{:S(2)}) collective-permute-start(bf16[128,288]{1,0:T(8,128)(2,1)S(1)} %add_convert_fusion.10), channel_id=1, source_target_pairs={{0,4},{1,5},{2,6},{3,7},{4,0},{5,1},{6,2},{7,3},{8,12},{9,13},{10,... | collective-permute-start | bytes 221192 | tf_op jit(solution)/shard_map/ppermute | solution.py:359
  29.3 10.8 %collective-permute-start.10 = (bf16[256,512]{1,0:T(8,128)(2,1)S(1)}, bf16[256,512]{1,0:T(8,128)(2,1)S(1)}, u32[]{:S(2)}, u32[]{:S(2)}) collective-permute-start(bf16[256,512]{1,0:T(8,128)(2,1)S(1)} %collective-permute-done.3.refs_0_), channel_id=1, source_target_pairs={{0,1},{1,0},{2,3},{3,2},{4,5},{5,4},{6,7},{7,6},{8,9},{9,8},{10,11... | collective-permute-start | bytes 786440 | tf_op jit(solution)/shard_map/ppermute | solution.py:355
  33.2 11.5 %collective-permute-start.6 = (bf16[128,288]{1,0:T(8,128)(2,1)S(1)}, bf16[128,288]{1,0:T(8,128)(2,1)S(1)}, u32[]{:S(2)}, u32[]{:S(2)}) collective-permute-start(bf16[128,288]{1,0:T(8,128)(2,1)S(1)} %add_convert_fusion.9), channel_id=1, source_target_pairs={{0,1},{1,0},{2,3},{3,2},{4,5},{5,4},{6,7},{7,6},{8,9},{9,8},{10,11... | collective-permute-start | bytes 221192 | tf_op jit(solution)/shard_map/ppermute | solution.py:355
  38.6 8.0 %collective-permute-start.9 = (bf16[256,512]{1,0:T(8,128)(2,1)S(1)}, bf16[256,512]{1,0:T(8,128)(2,1)S(1)}, u32[]{:S(2)}, u32[]{:S(2)}) collective-permute-start(bf16[256,512]{1,0:T(8,128)(2,1)S(1)} %collective-permute-done.5.refs_0_), channel_id=1, source_target_pairs={{0,1},{1,0},{2,3},{3,2},{4,5},{5,4},{6,7},{7,6},{8,9},{9,8},{10,11... | collective-permute-start | bytes 786440 | tf_op jit(solution)/shard_map/ppermute | solution.py:355
  73.7 8.6 %collective-permute-start.13 = (bf16[256,512]{1,0:T(8,128)(2,1)S(1)}, bf16[256,512]{1,0:T(8,128)(2,1)S(1)}, u32[]{:S(2)}, u32[]{:S(2)}) collective-permute-start(bf16[256,512]{1,0:T(8,128)(2,1)S(1)} %get-tuple-element.89), channel_id=1, source_target_pairs={{0,1},{1,0},{2,3},{3,2},{4,5},{5,4},{6,7},{7,6},{8,9},{9,8},{10,11... | collective-permute-start | bytes 786440 | tf_op jit(solution)/shard_map/ppermute | solution.py:355
  79.9 9.2 %collective-permute-start.16 = (bf16[256,512]{1,0:T(8,128)(2,1)S(1)}, bf16[256,512]{1,0:T(8,128)(2,1)S(1)}, u32[]{:S(2)}, u32[]{:S(2)}) collective-permute-start(bf16[256,512]{1,0:T(8,128)(2,1)S(1)} %get-tuple-element.91), channel_id=1, source_target_pairs={{0,1},{1,0},{2,3},{3,2},{4,5},{5,4},{6,7},{7,6},{8,9},{9,8},{10,11... | collective-permute-start | bytes 786440 | tf_op jit(solution)/shard_map/ppermute | solution.py:355
  80.8 14.0 %collective-permute-start.12 = (bf16[256,512]{1,0:T(8,128)(2,1)S(1)}, bf16[256,512]{1,0:T(8,128)(2,1)S(1)}, u32[]{:S(2)}, u32[]{:S(2)}) collective-permute-start(bf16[256,512]{1,0:T(8,128)(2,1)S(1)} %get-tuple-element.87), channel_id=1, source_target_pairs={{0,1},{1,0},{2,3},{3,2},{4,5},{5,4},{6,7},{7,6},{8,9},{9,8},{10,11... | collective-permute-start | bytes 786440 | tf_op jit(solution)/shard_map/ppermute | solution.py:355
  82.4 12.4 %collective-permute-start.14 = (bf16[256,512]{1,0:T(8,128)(2,1)S(1)}, bf16[256,512]{1,0:T(8,128)(2,1)S(1)}, u32[]{:S(2)}, u32[]{:S(2)}) collective-permute-start(bf16[256,512]{1,0:T(8,128)(2,1)S(1)} %add_convert_fusion.5), channel_id=1, source_target_pairs={{0,2},{1,3},{2,4},{3,5},{4,6},{5,7},{6,0},{7,1},{8,10},{9,11},{10,... | collective-permute-start | bytes 786440 | tf_op jit(solution)/shard_map/ppermute | solution.py:355
  82.4 17.1 %collective-permute-start.11 = (bf16[256,512]{1,0:T(8,128)(2,1)S(1)}, bf16[256,512]{1,0:T(8,128)(2,1)S(1)}, u32[]{:S(2)}, u32[]{:S(2)}) collective-permute-start(bf16[256,512]{1,0:T(8,128)(2,1)S(1)} %get-tuple-element.85), channel_id=1, source_target_pairs={{0,1},{1,0},{2,3},{3,2},{4,5},{5,4},{6,7},{7,6},{8,9},{9,8},{10,11... | collective-permute-start | bytes 786440 | tf_op jit(solution)/shard_map/ppermute | solution.py:355
  89.2 10.3 %collective-permute-start.17 = (bf16[256,512]{1,0:T(8,128)(2,1)S(1)}, bf16[256,512]{1,0:T(8,128)(2,1)S(1)}, u32[]{:S(2)}, u32[]{:S(2)}) collective-permute-start(bf16[256,512]{1,0:T(8,128)(2,1)S(1)} %add_convert_fusion.3), channel_id=1, source_target_pairs={{0,6},{1,7},{2,0},{3,1},{4,2},{5,3},{6,4},{7,5},{8,14},{9,15},{10,... | collective-permute-start | bytes 786440 | tf_op jit(solution)/shard_map/ppermute | solution.py:355
  94.9 8.6 %collective-permute-start.15 = (bf16[256,512]{1,0:T(8,128)(2,1)S(1)}, bf16[256,512]{1,0:T(8,128)(2,1)S(1)}, u32[]{:S(2)}, u32[]{:S(2)}) collective-permute-start(bf16[256,512]{1,0:T(8,128)(2,1)S(1)} %add_convert_fusion.4), channel_id=1, source_target_pairs={{0,2},{1,3},{2,4},{3,5},{4,6},{5,7},{6,0},{7,1},{8,10},{9,11},{10,... | collective-permute-start | bytes 786440 | tf_op jit(solution)/shard_map/ppermute | solution.py:355
  105.2 8.3 %collective-permute-start.19 = (bf16[256,512]{1,0:T(8,128)(2,1)S(1)}, bf16[256,512]{1,0:T(8,128)(2,1)S(1)}, u32[]{:S(2)}, u32[]{:S(2)}) collective-permute-start(bf16[256,512]{1,0:T(8,128)(2,1)S(1)} %fusion.3.refs_0_), channel_id=1, source_target_pairs={{0,2},{1,3},{2,4},{3,5},{4,6},{5,7},{6,0},{7,1},{8,10},{9,11},{10,... | collective-permute-start | bytes 786440 | tf_op jit(solution)/shard_map/ppermute | solution.py:355
  113.5 12.1 %collective-permute-start.21 = (bf16[256,512]{1,0:T(8,128)(2,1)S(1)}, bf16[256,512]{1,0:T(8,128)(2,1)S(1)}, u32[]{:S(2)}, u32[]{:S(2)}) collective-permute-start(bf16[256,512]{1,0:T(8,128)(2,1)S(1)} %fusion.3.refs_0_), channel_id=1, source_target_pairs={{0,6},{1,7},{2,0},{3,1},{4,2},{5,3},{6,4},{7,5},{8,14},{9,15},{10,... | collective-permute-start | bytes 786440 | tf_op jit(solution)/shard_map/ppermute | solution.py:355
  113.7 14.4 %collective-permute-start.26 = (bf16[256,512]{1,0:T(8,128)(2,1)S(1)}, bf16[256,512]{1,0:T(8,128)(2,1)S(1)}, u32[]{:S(2)}, u32[]{:S(2)}) collective-permute-start(bf16[256,512]{1,0:T(8,128)(2,1)S(1)} %fusion.3.refs_0_), channel_id=1, source_target_pairs={{0,1},{1,0},{2,3},{3,2},{4,5},{5,4},{6,7},{7,6},{8,9},{9,8},{10,11... | collective-permute-start | bytes 786440 | tf_op jit(solution)/shard_map/ppermute | solution.py:355
  115.3 19.7 %collective-permute-start.25 = (bf16[256,512]{1,0:T(8,128)(2,1)S(1)}, bf16[256,512]{1,0:T(8,128)(2,1)S(1)}, u32[]{:S(2)}, u32[]{:S(2)}) collective-permute-start(bf16[256,512]{1,0:T(8,128)(2,1)S(1)} %collective-permute-done.19.refs_0_), channel_id=1, source_target_pairs={{0,1},{1,0},{2,3},{3,2},{4,5},{5,4},{6,7},{7,6},{8,9},{9,8},{10,11... | collective-permute-start | bytes 786440 | tf_op jit(solution)/shard_map/ppermute | solution.py:355
  115.8 19.1 %collective-permute-start.23 = (bf16[256,512]{1,0:T(8,128)(2,1)S(1)}, bf16[256,512]{1,0:T(8,128)(2,1)S(1)}, u32[]{:S(2)}, u32[]{:S(2)}) collective-permute-start(bf16[256,512]{1,0:T(8,128)(2,1)S(1)} %collective-permute-done.19.refs_0_), channel_id=1, source_target_pairs={{0,2},{1,3},{2,4},{3,5},{4,6},{5,7},{6,0},{7,1},{8,10},{9,11},{10,... | collective-permute-start | bytes 786440 | tf_op jit(solution)/shard_map/ppermute | solution.py:355
  125.6 9.3 %collective-permute-start.22 = (bf16[128,288]{1,0:T(8,128)(2,1)S(1)}, bf16[128,288]{1,0:T(8,128)(2,1)S(1)}, u32[]{:S(2)}, u32[]{:S(2)}) collective-permute-start(bf16[128,288]{1,0:T(8,128)(2,1)S(1)} %add_convert_fusion.7), channel_id=1, source_target_pairs={{0,4},{1,5},{2,6},{3,7},{4,0},{5,1},{6,2},{7,3},{8,12},{9,13},{10,... | collective-permute-start | bytes 221192 | tf_op jit(solution)/shard_map/ppermute | solution.py:359
  132.8 9.3 %collective-permute-start.28 = (bf16[256,512]{1,0:T(8,128)(2,1)S(1)}, bf16[256,512]{1,0:T(8,128)(2,1)S(1)}, u32[]{:S(2)}, u32[]{:S(2)}) collective-permute-start(bf16[256,512]{1,0:T(8,128)(2,1)S(1)} %collective-permute-done.21.refs_0_), channel_id=1, source_target_pairs={{0,1},{1,0},{2,3},{3,2},{4,5},{5,4},{6,7},{7,6},{8,9},{9,8},{10,11... | collective-permute-start | bytes 786440 | tf_op jit(solution)/shard_map/ppermute | solution.py:355
  134.9 11.7 %collective-permute-start.24 = (bf16[128,288]{1,0:T(8,128)(2,1)S(1)}, bf16[128,288]{1,0:T(8,128)(2,1)S(1)}, u32[]{:S(2)}, u32[]{:S(2)}) collective-permute-start(bf16[128,288]{1,0:T(8,128)(2,1)S(1)} %add_convert_fusion.6), channel_id=1, source_target_pairs={{0,1},{1,0},{2,3},{3,2},{4,5},{5,4},{6,7},{7,6},{8,9},{9,8},{10,11... | collective-permute-start | bytes 221192 | tf_op jit(solution)/shard_map/ppermute | solution.py:355
  139.7 7.1 %collective-permute-start.27 = (bf16[256,512]{1,0:T(8,128)(2,1)S(1)}, bf16[256,512]{1,0:T(8,128)(2,1)S(1)}, u32[]{:S(2)}, u32[]{:S(2)}) collective-permute-start(bf16[256,512]{1,0:T(8,128)(2,1)S(1)} %collective-permute-done.23.refs_0_), channel_id=1, source_target_pairs={{0,1},{1,0},{2,3},{3,2},{4,5},{5,4},{6,7},{7,6},{8,9},{9,8},{10,11... | collective-permute-start | bytes 786440 | tf_op jit(solution)/shard_map/ppermute | solution.py:355
  173.7 8.7 %collective-permute-start.31 = (bf16[256,512]{1,0:T(8,128)(2,1)S(1)}, bf16[256,512]{1,0:T(8,128)(2,1)S(1)}, u32[]{:S(2)}, u32[]{:S(2)}) collective-permute-start(bf16[256,512]{1,0:T(8,128)(2,1)S(1)} %get-tuple-element.118), channel_id=1, source_target_pairs={{0,1},{1,0},{2,3},{3,2},{4,5},{5,4},{6,7},{7,6},{8,9},{9,8},{10,11... | collective-permute-start | bytes 786440 | tf_op jit(solution)/shard_map/ppermute | solution.py:355
  180.4 9.2 %collective-permute-start.34 = (bf16[256,512]{1,0:T(8,128)(2,1)S(1)}, bf16[256,512]{1,0:T(8,128)(2,1)S(1)}, u32[]{:S(2)}, u32[]{:S(2)}) collective-permute-start(bf16[256,512]{1,0:T(8,128)(2,1)S(1)} %get-tuple-element.120), channel_id=1, source_target_pairs={{0,1},{1,0},{2,3},{3,2},{4,5},{5,4},{6,7},{7,6},{8,9},{9,8},{10,11... | collective-permute-start | bytes 786440 | tf_op jit(solution)/shard_map/ppermute | solution.py:355
  180.8 14.4 %collective-permute-start.30 = (bf16[256,512]{1,0:T(8,128)(2,1)S(1)}, bf16[256,512]{1,0:T(8,128)(2,1)S(1)}, u32[]{:S(2)}, u32[]{:S(2)}) collective-permute-start(bf16[256,512]{1,0:T(8,128)(2,1)S(1)} %get-tuple-element.116), channel_id=1, source_target_pairs={{0,1},{1,0},{2,3},{3,2},{4,5},{5,4},{6,7},{7,6},{8,9},{9,8},{10,11... | collective-permute-start | bytes 786440 | tf_op jit(solution)/shard_map/ppermute | solution.py:355
  182.5 12.7 %collective-permute-start.32 = (bf16[256,512]{1,0:T(8,128)(2,1)S(1)}, bf16[256,512]{1,0:T(8,128)(2,1)S(1)}, u32[]{:S(2)}, u32[]{:S(2)}) collective-permute-start(bf16[256,512]{1,0:T(8,128)(2,1)S(1)} %add_convert_fusion.2), channel_id=1, source_target_pairs={{0,2},{1,3},{2,4},{3,5},{4,6},{5,7},{6,0},{7,1},{8,10},{9,11},{10,... | collective-permute-start | bytes 786440 | tf_op jit(solution)/shard_map/ppermute | solution.py:355
  183.6 16.3 %collective-permute-start.29 = (bf16[256,512]{1,0:T(8,128)(2,1)S(1)}, bf16[256,512]{1,0:T(8,128)(2,1)S(1)}, u32[]{:S(2)}, u32[]{:S(2)}) collective-permute-start(bf16[256,512]{1,0:T(8,128)(2,1)S(1)} %get-tuple-element.114), channel_id=1, source_target_pairs={{0,1},{1,0},{2,3},{3,2},{4,5},{5,4},{6,7},{7,6},{8,9},{9,8},{10,11... | collective-permute-start | bytes 786440 | tf_op jit(solution)/shard_map/ppermute | solution.py:355
  189.7 10.3 %collective-permute-start.35 = (bf16[256,512]{1,0:T(8,128)(2,1)S(1)}, bf16[256,512]{1,0:T(8,128)(2,1)S(1)}, u32[]{:S(2)}, u32[]{:S(2)}) collective-permute-start(bf16[256,512]{1,0:T(8,128)(2,1)S(1)} %add_convert_fusion), channel_id=1, source_target_pairs={{0,6},{1,7},{2,0},{3,1},{4,2},{5,3},{6,4},{7,5},{8,14},{9,15},{10,... | collective-permute-start | bytes 786440 | tf_op jit(solution)/shard_map/ppermute | solution.py:355
  195.3 8.4 %collective-permute-start.33 = (bf16[256,512]{1,0:T(8,128)(2,1)S(1)}, bf16[256,512]{1,0:T(8,128)(2,1)S(1)}, u32[]{:S(2)}, u32[]{:S(2)}) collective-permute-start(bf16[256,512]{1,0:T(8,128)(2,1)S(1)} %add_convert_fusion.1), channel_id=1, source_target_pairs={{0,2},{1,3},{2,4},{3,5},{4,6},{5,7},{6,0},{7,1},{8,10},{9,11},{10,... | collective-permute-start | bytes 786440 | tf_op jit(solution)/shard_map/ppermute | solution.py:355
  (13 other events, 161.2 us)
where the time goes:
time: 205 us
  Pallas kernels  80.7 us (39%)
  waiting for transfers between devices  62.2 us (30%)
  starting transfers between devices  43.2 us (21%)
  blocking collectives  10.9 us (5%)
  local copies, waits for them, and re-layouts  2.78 us (1%)
  other arithmetic  2.71 us (1%)
    ppermute x32, waiting for transfers between devices, send(): return lax.ppermute(value, 'tp', pairs)  58.2 us
    ppermute x32, starting transfers between devices, send(): return lax.ppermute(value, 'tp', pairs)  38.3 us
    pallas_call x8, Pallas kernels, project(): pl.pallas_call(functools.partial(proj_kernel, count, before is None, laye...  37.1 us
    pallas_call x2, Pallas kernels, local_scan(): pl.pallas_call(functools.partial(scan_kernel, layer, states, width), out_...  18.2 us
    pallas_call x2, Pallas kernels, close_layer(): pl.pallas_call(functools.partial(close_kernel, layer, states, table_at, f...  15.6 us
    all_gather x2, blocking collectives, per_device(): finals = lax.all_gather(final, 'seq')  10.9 us
    pallas_call x2, Pallas kernels, expand(): pl.pallas_call(functools.partial(expand_kernel, layer, table_at, feat), o...  9.81 us
    ppermute x4, starting transfers between devices, swap(): return lax.ppermute(value, 'tp', pairs)  4.92 us
  transfers between devices with their start and end apart: 36, of which 19 were waited for; matrix products, arithmetic and copies ran while one was open for 2% of the time, Pallas kernels for 18%

commit v1 on v0

--- a/solution.py
+++ b/solution.py
@@ -13,12 +13,14 @@
 STRIDE = 3
 EPS = 1e-05
 DEPTH = 4
-LIMIT = 40 * 1024 * 1024
+LIMIT = 28 * 1024 * 1024
 F32 = jnp.float32
 BF16 = jnp.bfloat16
 VMEM = pl.BlockSpec(memory_space=pltpu.VMEM)
 SMEM = pl.BlockSpec(memory_space=pltpu.SMEM)
 HBM = pl.BlockSpec(memory_space=pl.ANY)
+COST = pl.CostEstimate(flops=1, bytes_accessed=1, transcendentals=0)
+LONG = pl.CostEstimate(flops=10**10, bytes_accessed=1, transcendentals=0)
 
 
 def row_factor(square_sum, width):
@@ -33,102 +35,136 @@
     return pltpu.CompilerParams(vmem_limit_bytes=LIMIT)
 
 
-def proj_kernel(count, first, layer, table_at, depth, table_ref, *refs):
-    shards = refs[:count]
-    gain_ref, w_ref = refs[count : count + 2]
-    cur_ref, gate_ref, square_ref, raw_s, split_s, sems = refs[-6:]
-    rows, width = shards[0].shape
-    chans = cur_ref.shape[1]
+def unpack_kernel(count, layer, table_at, width, depth, table_ref, w_ref, *refs):
+    out_ref, token_ref, raw_s, split_s, sems = refs[-5:]
+    chans = out_ref.shape[2]
     per = 2 * chans // LANES
     pieces = width // depth
     size = depth * per
     apart = fold_stride(depth)
-    begins = [pl.multiple_of(table_ref[table_at + j] * width, width) for j in range(count)]
-
-    def copy(j, q):
-        n = j * pieces + q
-        return pltpu.make_async_copy(
-            w_ref.at[layer, pl.ds(pl.multiple_of((begins[j] + q * depth) * per, size), size), :],
-            raw_s.at[n],
-            sems.at[n],
-        )
-
-    for j in range(count):
-        for q in range(pieces):
-            copy(j, q).start()
-    squares = None if first else square_ref[...]
+    taken = max(per, 16)
+
+    def copy(n):
+        begin = table_ref[table_at + n // pieces] * width + (n % pieces) * depth
+        rows = pl.ds(pl.multiple_of(begin * per, size), size)
+        return pltpu.make_async_copy(w_ref.at[layer, rows, :], raw_s.at[n], sems.at[n])
+
+    for n in range(count * pieces):
+        copy(n).start()
+    token_ref[...] = jnp.zeros_like(token_ref)
+    for n in range(count * pieces):
+        copy(n).wait()
+        slot = n % 2
+
+        def spread(m, carried):
+            values = raw_s[n, pl.ds(pl.multiple_of(m * taken, taken), taken), :].astype(F32)
+            for k in range(taken // per):
+                d = m * (taken // per) + k
+                part = values[k * per : (k + 1) * per]
+                split_s[slot, pl.ds(d * STRIDE, per, stride=apart), :] = part
+            return carried
+
+        lax.fori_loop(0, size // taken, spread, 0, unroll=32)
+        for e in range(2):
+            for t in range(chans // LANES):
+                place = pl.ds((2 * t + e) * apart, depth, stride=STRIDE)
+                values = split_s[slot, place, :].astype(BF16)
+                out_ref[e, n * depth : (n + 1) * depth, t * LANES : (t + 1) * LANES] = values
+
+
+def unpack(layer, table, table_at, count, width, chans, w_raw, earlier):
+    depth = min(width, LANES)
+    pieces = count * width // depth
+    size = depth * 2 * chans // LANES
+    return pl.pallas_call(
+        functools.partial(unpack_kernel, count, layer, table_at, width, depth),
+        out_shape=[
+            jax.ShapeDtypeStruct((2, count * width, chans), BF16),
+            jax.ShapeDtypeStruct((8, LANES), F32),
+        ],
+        in_specs=[SMEM, HBM] + [HBM] * len(earlier),
+        out_specs=[VMEM, VMEM],
+        scratch_shapes=[
+            pltpu.VMEM((pieces, size, LANES), BF16),
+            pltpu.VMEM((2, 2 * chans // LANES * fold_stride(depth), LANES), F32),
+            pltpu.SemaphoreType.DMA((pieces,)),
+        ],
+        compiler_params=params(),
+        cost_estimate=COST,
+        name="unpack",
+    )(table, w_raw, *earlier)
+
+
+def proj_kernel(count, first, layer, table_at, table_ref, *refs):
+    shards = refs[:count]
+    gain_ref, w_ref = refs[count : count + 2]
+    cur_ref, gate_ref, square_ref = refs[-3:]
+    rows, width = shards[0].shape
+    chans = cur_ref.shape[1]
+    squares = jnp.zeros((rows, 1), F32) if first else square_ref[...]
+    parts = []
     for j in range(count):
         values = shards[j][...].astype(F32)
-        gain = gain_ref[layer : layer + 1, pl.ds(begins[j], width)]
-        scaled = (values * gain).astype(BF16)
-        term = jnp.sum(values * values, axis=1, keepdims=True)
-        squares = term if squares is None else squares + term
-        for q in range(pieces):
-            copy(j, q).wait()
-            slot = (j * pieces + q) % 2
-            raw = raw_s.at[j * pieces + q]
-
-            def spread(n, carried):
-                taken = max(per, 16)
-                values = raw[pl.ds(pl.multiple_of(n * taken, taken), taken), :].astype(F32)
-                for k in range(taken // per):
-                    d = n * (taken // per) + k
-                    part = values[k * per : (k + 1) * per]
-                    split_s[slot, pl.ds(d * STRIDE, per, stride=apart), :] = part
-                return carried
-
-            lax.fori_loop(0, size // max(per, 16), spread, 0, unroll=16)
-            left = scaled[:, q * depth : (q + 1) * depth]
-            for e, out in enumerate((cur_ref, gate_ref)):
-                for begin in range(0, chans, WIDE):
-                    tiles = [
-                        split_s[slot, pl.ds((2 * t + e) * apart, depth, stride=STRIDE), :].astype(BF16)
-                        for t in range(begin // LANES, (begin + WIDE) // LANES)
-                    ]
-                    product = jnp.dot(
-                        left, jnp.concatenate(tiles, axis=1), preferred_element_type=F32
-                    )
-                    cols = slice(begin, begin + WIDE)
-                    if first and j == 0 and q == 0:
-                        out[:, cols] = product
-                    else:
-                        out[:, cols] += product
+        begin = pl.multiple_of(table_ref[table_at + j] * width, width)
+        parts.append((values * gain_ref[layer : layer + 1, pl.ds(begin, width)]).astype(BF16))
+        squares = squares + jnp.sum(values * values, axis=1, keepdims=True)
     square_ref[...] = squares
-
-
-def project(layer, shards, table, table_at, norm_gain, w_raw, chans, before):
+    left = jnp.concatenate(parts, axis=1)
+    for e, out in enumerate((cur_ref, gate_ref)):
+        for begin in range(0, chans, WIDE):
+            cols = slice(begin, begin + WIDE)
+            product = jnp.dot(left, w_ref[e, :, cols], preferred_element_type=F32)
+            if first:
+                out[:, cols] = product
+            else:
+                out[:, cols] += product
+
+
+def project(layer, shards, table, table_at, norm_gain, w_lanes, before, earlier):
     count = len(shards)
     rows, width = shards[0].shape
-    depth = min(width, WIDE)
-    pieces = count * (width // depth)
-    size = depth * 2 * chans // LANES
+    chans = w_lanes.shape[2]
     state = [jax.ShapeDtypeStruct(s, F32) for s in ((rows, chans), (rows, chans), (rows, 1))]
-    operands = [table, *shards, norm_gain, w_raw]
-    in_specs = [SMEM] + [VMEM] * (count + 1) + [HBM]
+    operands = [table, *shards, norm_gain, w_lanes]
+    in_specs = [SMEM] + [VMEM] * (count + 2)
     aliases = {}
     if before is not None:
         aliases = {len(operands) + j: j for j in range(3)}
         in_specs += [VMEM] * 3
         operands += list(before)
+    in_specs += [HBM] * len(earlier)
+    operands += earlier
     return pl.pallas_call(
-        functools.partial(proj_kernel, count, before is None, layer, table_at, depth),
+        functools.partial(proj_kernel, count, before is None, layer, table_at),
         out_shape=state,
         in_specs=in_specs,
         out_specs=[VMEM] * 3,
-        scratch_shapes=[
-            pltpu.VMEM((pieces, size, LANES), BF16),
-            pltpu.VMEM((2, 2 * chans // LANES * fold_stride(depth), LANES), F32),
-            pltpu.SemaphoreType.DMA((pieces,)),
-        ],
         input_output_aliases=aliases,
         compiler_params=params(),
-        cost_estimate=pl.CostEstimate(
-            flops=4 * count * rows * width * chans,
-            bytes_accessed=count * (4 * width * chans + 2 * rows * width),
-            transcendentals=0,
-        ),
+        cost_estimate=LONG,
         name="project",
     )(*operands)
+
+
+def low_kernel(layer, table_ref, rows_ref, gain_ref, w_ref, *refs):
+    width = rows_ref.shape[1]
+    begin = pl.multiple_of(table_ref[0] * width, width)
+    gain = gain_ref[layer : layer + 1, pl.ds(begin, width)]
+    scaled = (rows_ref[...].astype(F32) * gain).astype(BF16)
+    product = jnp.dot(scaled, w_ref[layer], preferred_element_type=F32)
+    refs[-1][...] = product.astype(BF16)
+
+
+def project_low(layer, table, own_rows, norm_gain, w_low, earlier):
+    return pl.pallas_call(
+        functools.partial(low_kernel, layer),
+        out_shape=jax.ShapeDtypeStruct((own_rows.shape[0], w_low.shape[2]), BF16),
+        in_specs=[SMEM] + [VMEM] * 3 + [HBM] * len(earlier),
+        out_specs=VMEM,
+        compiler_params=params(),
+        cost_estimate=COST,
+        name="project_low",
+    )(table, own_rows, norm_gain, w_low, *earlier)
 
 
 def scan_kernel(
@@ -207,11 +243,7 @@
         out_specs=[VMEM] * 3,
         scratch_shapes=[pltpu.VMEM(folded, F32), pltpu.VMEM(folded, F32)],
         compiler_params=params(),
-        cost_estimate=pl.CostEstimate(
-            flops=8 * rows * states * chans,
-            bytes_accessed=20 * rows * chans,
-            transcendentals=rows * states * chans,
-        ),
+        cost_estimate=COST,
         name="local_scan",
     )(selectors, low, square, cur, w_dt, dt_bias, rate)
 
@@ -302,11 +334,7 @@
             pltpu.SemaphoreType.DMA((count,)),
         ],
         compiler_params=params(),
-        cost_estimate=pl.CostEstimate(
-            flops=6 * rows * states * chans + 2 * count * rows * chans * feat,
-            bytes_accessed=20 * rows * chans + 2 * count * chans * feat,
-            transcendentals=rows * states * chans,
-        ),
+        cost_estimate=COST,
         name="close_layer",
     )(table, seq_place, selectors, *values, rate, skip, thresh, w_out)
     return results[0], results[1:]
@@ -330,11 +358,7 @@
             pltpu.SemaphoreType.DMA((count,)),
         ],
         compiler_params=params(),
-        cost_estimate=pl.CostEstimate(
-            flops=2 * count * rows * chans * feat,
-            bytes_accessed=2 * count * chans * feat + 2 * (count + 2) * rows * feat,
-            transcendentals=0,
-        ),
+        cost_estimate=COST,
         name="expand",
     )(table, gated, w_out)
 
@@ -370,10 +394,6 @@
         return jnp.concatenate(both).astype(jnp.int32)
 
 
-def after(value, *others):
-    return lax.optimization_barrier((value, others))[0]
-
-
 def gather_columns(grid, own):
     columns = {0: own}
     half = grid.depth // 2
@@ -394,7 +414,7 @@
     return order + [0]
 
 
-def scatter_sum(grid, own_rows, chunks):
+def scatter_sum(grid, own_rows, chunks, aside):
     crossed = {
         (a, b): grid.send(chunks[a, b], 0, b)
         for a in scatter_order(grid)
@@ -402,10 +422,15 @@
     }
     half = grid.depth - grid.depth // 2
     arriving = {}
+    waiting = ()
     for a in scatter_order(grid):
         part = chunks[a, 0].astype(F32)
         for b in range(1, grid.side):
             part = part + crossed[a, b].astype(F32)
+        others = waiting
+        waiting = aside(a, crossed.get((a, 1), chunks[a, 0]))
+        for token in others:
+            part = part + token[0, 0]
         if a == 0:
             total = own_rows.astype(F32) + part
         elif a <= half:
@@ -415,12 +440,14 @@
         else:
             if a in arriving:
                 part = part + arriving[a].astype(F32)
-            after = (a + 1) % grid.depth
+            target = (a + 1) % grid.depth
             moved = grid.send(part.astype(BF16), -1, 0)
-            if after == 0:
+            if target == 0:
                 last = moved
             else:
-                arriving[after] = moved
+                arriving[target] = moved
+    for token in waiting:
+        total = total + token[0, 0]
     if grid.depth > 1:
         total = total + arriving[0].astype(F32)
     if grid.depth > 2:
@@ -428,8 +455,7 @@
     return total.astype(BF16)
 
 
-def sum_selectors(grid, partial, arrivals):
-    arrivals = list(arrivals)
+def sum_selectors(grid, partial):
     rows = partial.shape[0]
     part = rows // grid.side
     own_y = lax.axis_index("tp") % grid.side
@@ -438,17 +464,20 @@
     for b in range(1, grid.side):
         total = total + grid.send(piece(own_y + b), 0, b).astype(F32)
     bit = 1
+    stages = []
     while bit < grid.depth:
-        total = after(total.astype(BF16), arrivals.pop(0))
+        total = total.astype(BF16)
+        stages.append(total)
         total = total.astype(F32) + grid.swap(total, bit).astype(F32)
         bit *= 2
-    total = after(total.astype(BF16), arrivals.pop(0))
+    total = total.astype(BF16)
+    stages.append(total)
     result = jnp.zeros_like(partial)
     for b in range(grid.side):
         got = grid.send(total, 0, b) if b else total
         place = ((own_y - b + grid.side) % grid.side) * part
         result = lax.dynamic_update_slice_in_dim(result, got, place, 0)
-    return result
+    return result, stages
 
 
 def per_device(
@@ -463,29 +492,37 @@
     table = grid.table()
     forth = lambda a, b: n_tp + a * grid.side + b
     seq_place = lax.axis_index("seq").astype(jnp.int32).reshape(1)
-    own_place = lax.axis_index("tp") * feat
     rates = (a_rate * (-math.log2(math.e))).reshape(layers, states, fold, LANES)
     w_raw = w_in.reshape(layers, width, 2, fold, LANES).transpose(0, 1, 3, 2, 4)
     w_raw = w_raw.reshape(layers, width * 2 * fold, LANES)
-    own_gain = lax.dynamic_slice_in_dim(norm_gain, own_place, feat, 1)
     order = scatter_order(grid)
     own_rows = tokens
+    open_weights = lambda layer, a, earlier: unpack(
+        layer, table, a * grid.side, grid.side, feat, chans, w_raw, earlier
+    )
+    weights = {}
+    arrivals = order[::-1]
     for layer in range(layers):
         columns = gather_columns(grid, own_rows)
-        arrivals = order[::-1]
-        scaled = (own_rows.astype(F32) * own_gain[layer]).astype(BF16)
-        low = jnp.dot(scaled, w_low[layer], preferred_element_type=F32).astype(BF16)
-        low = sum_selectors(grid, low, [columns[a] for a in arrivals[1:]])
+        across = {
+            a: [columns[a]] + [grid.send(columns[a], 0, b) for b in range(1, grid.side)]
+            for a in arrivals
+        }
+        earlier = [*across[0][1:], columns[arrivals[1]]]
+        if not weights:
+            weights[0], token = open_weights(layer, 0, [])
+            earlier.append(token)
+        low = project_low(layer, table, own_rows, norm_gain, w_low, earlier)
+        low, stages = sum_selectors(grid, low)
         selectors = low[:, rank:].astype(F32)
         state = None
-        squares = []
         for n, a in enumerate(arrivals):
-            column = after(columns[a], squares[n - 2]) if n > 1 else columns[a]
-            arrived = [column] + [grid.send(column, 0, b) for b in range(1, grid.side)]
+            if a not in weights:
+                weights[a], _ = open_weights(layer, a, across[arrivals[n - 1]][1:])
+            earlier = stages[n - 1 : n] if n else []
             state = project(
-                layer, arrived, table, a * grid.side, norm_gain, w_raw, chans, state
+                layer, across[a], table, a * grid.side, norm_gain, weights[a], state, earlier
             )
-            squares.append(state[2])
         cur, gate, square = state
         out, time, final = local_scan(
             layer, width, selectors, low, square, cur, w_dt, dt_bias, rates
@@ -509,7 +546,17 @@
             w_out,
         )
         others = expand(layer, table, [forth(*key) for key in keys[lead:]], feat, gated, w_out)
-        own_rows = scatter_sum(grid, own_rows, dict(zip(keys, [*chunks, *others])))
+        coming = {}
+
+        def aside(a, value):
+            if layer + 1 == layers:
+                return ()
+            a = grid.depth - 1 - a
+            coming[a], token = open_weights(layer + 1, a, [value])
+            return (token,)
+
+        own_rows = scatter_sum(grid, own_rows, dict(zip(keys, [*chunks, *others])), aside)
+        weights = coming
     return own_rows
 
 

time: 205 us -> 231 us (1.13)
  local copies, waits for them, and re-layouts: 2.78 us -> 29.9 us
  Pallas kernels: 80.7 us -> 92.4 us
  waiting for transfers between devices: 62.2 us -> 52.2 us
  starting transfers between devices: 43.2 us -> 40.3 us
    pallas_call x0 -> x10, Pallas kernels: none -> 34.4 us  [the longest x8 32.7 us: unpack(): pl.pallas_call(functools.partial(unpack_kernel, count, layer, table_at, w...]
    unnamed x19 -> x30, local copies, waits for them, and re-layouts: 1.77 us -> 27.7 us
    pallas_call x8, Pallas kernels: 37.1 us -> 14.5 us  [project(): pl.pallas_call(functools.partial(proj_kernel, count, before is None, laye...]
    ppermute x32, waiting for transfers between devices: 58.2 us -> 38.3 us  [send(): return lax.ppermute(value, 'tp', pairs)]
    ppermute x4, waiting for transfers between devices: 4 us -> 13.9 us  [swap(): return lax.ppermute(value, 'tp', pairs)]
    ppermute x4, starting transfers between devices: 4.92 us -> 1.41 us  [swap(): return lax.ppermute(value, 'tp', pairs)]
  transfers between devices with their start and end apart: 36 -> 36, of which waited for: 19 -> 16; matrix products, arithmetic and copies ran while one was open for 2% -> 2% of each run, Pallas kernels for 18% -> 23%
where the time goes in v1:
time: 231 us
  Pallas kernels  92.4 us (40%)
  waiting for transfers between devices  52.2 us (23%)
  starting transfers between devices  40.3 us (17%)
  local copies, waits for them, and re-layouts  29.9 us (13%)
  blocking collectives  10.9 us (5%)
  other arithmetic  4.46 us (2%)
    ppermute x32, starting transfers between devices, send(): return lax.ppermute(value, 'tp', pairs)  38.9 us
    ppermute x32, waiting for transfers between devices, send(): return lax.ppermute(value, 'tp', pairs)  38.3 us
    pallas_call x8, Pallas kernels, unpack(): pl.pallas_call(functools.partial(unpack_kernel, count, layer, table_at, w...  32.7 us
    unnamed x30, local copies, waits for them, and re-layouts  27.7 us
    pallas_call x2, Pallas kernels, local_scan(): pl.pallas_call(functools.partial(scan_kernel, layer, states, width), out_...  18.2 us
    pallas_call x2, Pallas kernels, close_layer(): pl.pallas_call(functools.partial(close_kernel, layer, states, table_at, f...  16 us
    pallas_call x8, Pallas kernels, project(): pl.pallas_call(functools.partial(proj_kernel, count, before is None, laye...  14.5 us
    ppermute x4, waiting for transfers between devices, swap(): return lax.ppermute(value, 'tp', pairs)  13.9 us
  transfers between devices with their start and end apart: 36, of which 16 were waited for; matrix products, arithmetic and copies ran while one was open for 2% of the time, Pallas kernels for 23%

profile of v1, /device:TPU:0, one launch (start us, length us, event | category | flops | bytes accessed | tf_op | source)
XLA Modules:
  0.0 230.7 jit_solution(319655509963170245)
XLA Ops:
  0.0 3.0 %collective-permute-start = (bf16[256,512]{1,0:T(8,128)(2,1)}, bf16[256,512]{1,0:T(8,128)(2,1)S(1)}, u32[]{:S(2)}, u32[]{:S(2)}) collective-permute-start(bf16[256,512]{1,0:T(8,128)(2,1)} %refs_0_.1), channel_id=1, source_target_pairs={{0,1},{1,0},{2,3},{3,2},{4,5},{5,4},{6,7},{7,6},{8,9},{9,8},{10,11... | collective-permute-start | bytes 786440 | tf_op jit(solution)/shard_map/ppermute | solution.py:379
  4.6 3.9 %unpack.8 = (bf16[2,1024,1024]{2,1,0:T(8,128)(2,1)S(1)}, f32[8,128]{1,0:T(8,128)S(1)}) custom-call(s32[16]{0:T(128)S(1)} %pad_add_fusion.table_ref, bf16[2,65536,128]{2,1,0:T(8,128)(2,1)} %bitcast.22), custom_call_target="tpu_custom_call" | custom-call | flops 1 | bytes 1 | tf_op jit(solution)/shard_map/unpack/pallas_call | solution.py:79
  21.2 6.3 %collective-permute-done.3 = bf16[128,288]{1,0:T(8,128)(2,1)S(1)} collective-permute-done((bf16[128,288]{1,0:T(8,128)(2,1)S(1)}, bf16[128,288]{1,0:T(8,128)(2,1)S(1)}, u32[]{:S(2)}, u32[]{:S(2)}) %collective-permute-start.3) | collective-permute-done | bytes 73760 | tf_op jit(solution)/shard_map/ppermute | solution.py:383
  31.6 4.4 %unpack.11 = (bf16[2,1024,1024]{2,1,0:T(8,128)(2,1)S(1)}, f32[8,128]{1,0:T(8,128)}) custom-call(s32[16]{0:T(128)S(1)} %pad_add_fusion.table_ref, bf16[2,65536,128]{2,1,0:T(8,128)(2,1)} %bitcast.23, bf16[256,512]{1,0:T(8,128)(2,1)S(1)} %collective-permute-done.refs_0_.refs_1_), custom_call_target="tpu_custom_call" | custom-call | flops 1 | bytes 1 | tf_op jit(solution)/shard_map/unpack/pallas_call | solution.py:79
  41.5 4.4 %unpack.10 = (bf16[2,1024,1024]{2,1,0:T(8,128)(2,1)S(1)}, f32[8,128]{1,0:T(8,128)}) custom-call(s32[16]{0:T(128)S(1)} %pad_add_fusion.table_ref, bf16[2,65536,128]{2,1,0:T(8,128)(2,1)} %bitcast.24, bf16[256,512]{1,0:T(8,128)(2,1)S(1)} %collective-permute-done.10.refs_0_.refs_1_), custom_call_target="tpu_custom_call" | custom-call | flops 1 | bytes 1 | tf_op jit(solution)/shard_map/unpack/pallas_call | solution.py:79
  47.7 4.4 %unpack.9 = (bf16[2,1024,1024]{2,1,0:T(8,128)(2,1)S(1)}, f32[8,128]{1,0:T(8,128)}) custom-call(s32[16]{0:T(128)S(1)} %pad_add_fusion.table_ref, bf16[2,65536,128]{2,1,0:T(8,128)(2,1)} %bitcast.25, bf16[256,512]{1,0:T(8,128)(2,1)S(1)} %collective-permute-done.9.refs_0_.refs_1_), custom_call_target="tpu_custom_call" | custom-call | flops 1 | bytes 1 | tf_op jit(solution)/shard_map/unpack/pallas_call | solution.py:79
  54.0 9.1 %local_scan.2 = (f32[6152,128]{1,0:T(8,128)S(1)}, f32[6152,128]{1,0:T(8,128)S(1)}, bf16[17,8,128]{2,1,0:T(8,128)(2,1)S(1)}) custom-call(f32[256,32]{1,0:T(8,128)S(1)} %slice_convert_fusion.1.sel_ref, bf16[256,288]{1,0:T(8,128)(2,1)S(1)} %constant_dynamic-update-slice_fusion.2.low_ref, f32[256,1]{1,0:T(8,128)S(1)} %get-tuple-element.80.square_ref.refs_4_, ...), custom_call_target="tpu_custom_call" | custom-call | flops 1 | bytes 1 | tf_op jit(solution)/shard_map/local_scan/pallas_call | solution.py:235
  63.1 5.4 %all-gather = bf16[68,8,128]{2,1,0:T(8,128)(2,1)S(1)} all-gather(bf16[17,8,128]{2,1,0:T(8,128)(2,1)S(1)} %get-tuple-element.85), channel_id=2, replica_groups=mesh['seq'=4,'tp'=8] {'seq'}, dimensions={0}, use_global_device_ids=true | all-gather | bytes 174080 | tf_op jit(solution)/shard_map/all_gather | solution.py:530
  68.6 5.8 %copy-done = bf16[2,1024,4096]{2,1,0:T(8,128)(2,1)S(1)} copy-done((bf16[2,1024,4096]{2,1,0:T(8,128)(2,1)S(1)}, bf16[2,1024,4096]{2,1,0:T(8,128)(2,1)}, u32[]{:S(2)}) %copy-start) | copy-done | bytes 16777240
  74.4 8.1 %close_layer.2 = (bf16[256,1024]{1,0:T(8,128)(2,1)S(1)}, bf16[256,512]{1,0:T(8,128)(2,1)S(1)}) custom-call(s32[16]{0:T(128)S(1)} %pad_add_fusion.table_ref, s32[1]{0:T(128)} %bitcast.place_ref, f32[256,32]{1,0:T(8,128)S(1)} %slice_convert_fusion.1.sel_ref, f32[6152,128]{1,0:T(8,128)S(1)} %get-tuple-element.82.refs_0_, ...), custom_call_target="tpu_custom_call" | custom-call | flops 1 | bytes 1 | tf_op jit(solution)/shard_map/close_layer/pallas_call | solution.py:325
  83.2 5.8 %copy-done.1 = bf16[2,1024,4096]{2,1,0:T(8,128)(2,1)S(1)} copy-done((bf16[2,1024,4096]{2,1,0:T(8,128)(2,1)S(1)}, bf16[2,1024,4096]{2,1,0:T(8,128)(2,1)}, u32[]{:S(2)}) %copy-start.1) | copy-done | bytes 16777240
  88.9 4.7 %expand.2 = (bf16[256,512]{1,0:T(8,128)(2,1)S(1)}, bf16[256,512]{1,0:T(8,128)(2,1)S(1)}, bf16[256,512]{1,0:T(8,128)(2,1)S(1)}, bf16[256,512]{1,0:T(8,128)(2,1)S(...) custom-call(s32[16]{0:T(128)S(1)} %pad_add_fusion.table_ref, ...), custom_call_target="tpu_custom_call" | custom-call | flops 1 | bytes 1 | tf_op jit(solution)/shard_map/expand/pallas_call | solution.py:351
  97.5 3.9 %unpack.15 = (bf16[2,1024,1024]{2,1,0:T(8,128)(2,1)S(1)}, f32[8,128]{1,0:T(8,128)S(1)}) custom-call(s32[16]{0:T(128)S(1)} %pad_add_fusion.table_ref, bf16[2,65536,128]{2,1,0:T(8,128)(2,1)} %bitcast.26, bf16[256,512]{1,0:T(8,128)(2,1)S(1)} %collective-permute-done.14.refs_0_), custom_call_target="tpu_custom_call" | custom-call | flops 1 | bytes 1 | tf_op jit(solution)/shard_map/unpack/pallas_call | solution.py:79
  102.8 3.9 %unpack.14 = (bf16[2,1024,1024]{2,1,0:T(8,128)(2,1)S(1)}, f32[8,128]{1,0:T(8,128)S(1)}) custom-call(s32[16]{0:T(128)S(1)} %pad_add_fusion.table_ref, bf16[2,65536,128]{2,1,0:T(8,128)(2,1)} %bitcast.27, bf16[256,512]{1,0:T(8,128)(2,1)S(1)} %collective-permute-done.13.refs_0_), custom_call_target="tpu_custom_call" | custom-call | flops 1 | bytes 1 | tf_op jit(solution)/shard_map/unpack/pallas_call | solution.py:79
  111.6 3.9 %unpack.12 = (bf16[2,1024,1024]{2,1,0:T(8,128)(2,1)S(1)}, f32[8,128]{1,0:T(8,128)S(1)}) custom-call(s32[16]{0:T(128)S(1)} %pad_add_fusion.table_ref, bf16[2,65536,128]{2,1,0:T(8,128)(2,1)} %bitcast.28, bf16[256,512]{1,0:T(8,128)(2,1)S(1)} %collective-permute-done.12.refs_0_), custom_call_target="tpu_custom_call" | custom-call | flops 1 | bytes 1 | tf_op jit(solution)/shard_map/unpack/pallas_call | solution.py:79
  115.5 3.9 %unpack.13 = (bf16[2,1024,1024]{2,1,0:T(8,128)(2,1)S(1)}, f32[8,128]{1,0:T(8,128)S(1)}) custom-call(s32[16]{0:T(128)S(1)} %pad_add_fusion.table_ref, bf16[2,65536,128]{2,1,0:T(8,128)(2,1)} %bitcast.29, bf16[256,512]{1,0:T(8,128)(2,1)S(1)} %collective-permute-done.11.refs_0_), custom_call_target="tpu_custom_call" | custom-call | flops 1 | bytes 1 | tf_op jit(solution)/shard_map/unpack/pallas_call | solution.py:79
  120.5 2.6 %collective-permute-done.16 = bf16[256,512]{1,0:T(8,128)(2,1)S(1)} collective-permute-done((bf16[256,512]{1,0:T(8,128)(2,1)S(1)}, bf16[256,512]{1,0:T(8,128)(2,1)S(1)}, u32[]{:S(2)}, u32[]{:S(2)}) %collective-permute-start.16) | collective-permute-done | bytes 262176 | tf_op jit(solution)/shard_map/ppermute | solution.py:379
  126.1 5.0 %collective-permute-done.18.refs_0_.refs_1_ = bf16[256,512]{1,0:T(8,128)(2,1)S(1)} collective-permute-done((bf16[256,512]{1,0:T(8,128)(2,1)S(1)}, bf16[256,512]{1,0:T(8,128)(2,1)S(1)}, u32[]{:S(2)}, u32[]{:S(2)}) %collective-permute-start.18) | collective-permute-done | bytes 262176 | tf_op jit(solution)/shard_map/ppermute | solution.py:379
  131.0 3.2 %collective-permute-done.19.refs_1_.refs_0_ = bf16[256,512]{1,0:T(8,128)(2,1)S(1)} collective-permute-done((bf16[256,512]{1,0:T(8,128)(2,1)S(1)}, bf16[256,512]{1,0:T(8,128)(2,1)S(1)}, u32[]{:S(2)}, u32[]{:S(2)}) %collective-permute-start.19) | collective-permute-done | bytes 262176 | tf_op jit(solution)/shard_map/ppermute | solution.py:379
  136.0 3.8 %collective-permute-done.20 = bf16[128,288]{1,0:T(8,128)(2,1)S(1)} collective-permute-done((bf16[128,288]{1,0:T(8,128)(2,1)S(1)}, bf16[128,288]{1,0:T(8,128)(2,1)S(1)}, u32[]{:S(2)}, u32[]{:S(2)}) %collective-permute-start.20) | collective-permute-done | bytes 73760 | tf_op jit(solution)/shard_map/ppermute | solution.py:379
  143.1 3.5 %collective-permute-done.21 = bf16[128,288]{1,0:T(8,128)(2,1)S(1)} collective-permute-done((bf16[128,288]{1,0:T(8,128)(2,1)S(1)}, bf16[128,288]{1,0:T(8,128)(2,1)S(1)}, u32[]{:S(2)}, u32[]{:S(2)}) %collective-permute-start.21) | collective-permute-done | bytes 73760 | tf_op jit(solution)/shard_map/ppermute | solution.py:383
  152.5 4.1 %collective-permute-done.22 = bf16[128,288]{1,0:T(8,128)(2,1)S(1)} collective-permute-done((bf16[128,288]{1,0:T(8,128)(2,1)S(1)}, bf16[128,288]{1,0:T(8,128)(2,1)S(1)}, u32[]{:S(2)}, u32[]{:S(2)}) %collective-permute-start.22) | collective-permute-done | bytes 73760 | tf_op jit(solution)/shard_map/ppermute | solution.py:383
  166.4 9.1 %local_scan.3 = (f32[6152,128]{1,0:T(8,128)S(1)}, f32[6152,128]{1,0:T(8,128)S(1)}, bf16[17,8,128]{2,1,0:T(8,128)(2,1)S(1)}) custom-call(f32[256,32]{1,0:T(8,128)S(1)} %slice_convert_fusion.sel_ref, bf16[256,288]{1,0:T(8,128)(2,1)S(1)} %constant_dynamic-update-slice_fusion.low_ref, f32[256,1]{1,0:T(8,128)S(1)} %get-tuple-element.112.square_ref.refs_4_, ...), custom_call_target="tpu_custom_call" | custom-call | flops 1 | bytes 1 | tf_op jit(solution)/shard_map/local_scan/pallas_call | solution.py:235
  175.5 5.4 %all-gather.1 = bf16[68,8,128]{2,1,0:T(8,128)(2,1)S(1)} all-gather(bf16[17,8,128]{2,1,0:T(8,128)(2,1)S(1)} %get-tuple-element.117), channel_id=3, replica_groups=mesh['seq'=4,'tp'=8] {'seq'}, dimensions={0}, use_global_device_ids=true | all-gather | bytes 174080 | tf_op jit(solution)/shard_map/all_gather | solution.py:530
  181.0 5.8 %copy-done.2 = bf16[2,1024,4096]{2,1,0:T(8,128)(2,1)S(1)} copy-done((bf16[2,1024,4096]{2,1,0:T(8,128)(2,1)S(1)}, bf16[2,1024,4096]{2,1,0:T(8,128)(2,1)}, u32[]{:S(2)}) %copy-start.2) | copy-done | bytes 16777240
  186.7 7.9 %close_layer.3 = (bf16[256,1024]{1,0:T(8,128)(2,1)S(1)}, bf16[256,512]{1,0:T(8,128)(2,1)S(1)}) custom-call(s32[16]{0:T(128)S(1)} %pad_add_fusion.table_ref, s32[1]{0:T(128)} %bitcast.place_ref, f32[256,32]{1,0:T(8,128)S(1)} %slice_convert_fusion.sel_ref, f32[6152,128]{1,0:T(8,128)S(1)} %get-tuple-element.114.refs_0_, ...), custom_call_target="tpu_custom_call" | custom-call | flops 1 | bytes 1 | tf_op jit(solution)/shard_map/close_layer/pallas_call | solution.py:325
  196.0 5.8 %copy-done.3 = bf16[2,1024,4096]{2,1,0:T(8,128)(2,1)S(1)} copy-done((bf16[2,1024,4096]{2,1,0:T(8,128)(2,1)S(1)}, bf16[2,1024,4096]{2,1,0:T(8,128)(2,1)}, u32[]{:S(2)}) %copy-start.3) | copy-done | bytes 16777240
  201.8 4.7 %expand.3 = (bf16[256,512]{1,0:T(8,128)(2,1)S(1)}, bf16[256,512]{1,0:T(8,128)(2,1)S(1)}, bf16[256,512]{1,0:T(8,128)(2,1)S(1)}, bf16[256,512]{1,0:T(8,128)(2,1)S(...) custom-call(s32[16]{0:T(128)S(1)} %pad_add_fusion.table_ref, ...), custom_call_target="tpu_custom_call" | custom-call | flops 1 | bytes 1 | tf_op jit(solution)/shard_map/expand/pallas_call | solution.py:351
  211.5 4.2 %collective-permute-done.34 = bf16[256,512]{1,0:T(8,128)(2,1)S(1)} collective-permute-done((bf16[256,512]{1,0:T(8,128)(2,1)S(1)}, bf16[256,512]{1,0:T(8,128)(2,1)S(1)}, u32[]{:S(2)}, u32[]{:S(2)}) %collective-permute-start.34) | collective-permute-done | bytes 262176 | tf_op jit(solution)/shard_map/ppermute | solution.py:379
  218.1 3.2 %collective-permute-done.30 = bf16[256,512]{1,0:T(8,128)(2,1)S(1)} collective-permute-done((bf16[256,512]{1,0:T(8,128)(2,1)S(1)}, bf16[256,512]{1,0:T(8,128)(2,1)S(1)}, u32[]{:S(2)}, u32[]{:S(2)}) %collective-permute-start.30) | collective-permute-done | bytes 262176 | tf_op jit(solution)/shard_map/ppermute | solution.py:379
  222.8 3.2 %collective-permute-done.29 = bf16[256,512]{1,0:T(8,128)(2,1)S(1)} collective-permute-done((bf16[256,512]{1,0:T(8,128)(2,1)S(1)}, bf16[256,512]{1,0:T(8,128)(2,1)S(1)}, u32[]{:S(2)}, u32[]{:S(2)}) %collective-permute-start.29) | collective-permute-done | bytes 262176 | tf_op jit(solution)/shard_map/ppermute | solution.py:379
  226.1 3.8 %collective-permute-done.33 = bf16[256,512]{1,0:T(8,128)(2,1)S(1)} collective-permute-done((bf16[256,512]{1,0:T(8,128)(2,1)S(1)}, bf16[256,512]{1,0:T(8,128)(2,1)S(1)}, u32[]{:S(2)}, u32[]{:S(2)}) %collective-permute-start.33) | collective-permute-done | bytes 262176 | tf_op jit(solution)/shard_map/ppermute | solution.py:379
  (125 shorter events, 74.2 us)
Async XLA Ops:
  0.0 10.9 %collective-permute-start = (bf16[256,512]{1,0:T(8,128)(2,1)}, bf16[256,512]{1,0:T(8,128)(2,1)S(1)}, u32[]{:S(2)}, u32[]{:S(2)}) collective-permute-start(bf16[256,512]{1,0:T(8,128)(2,1)} %refs_0_.1), channel_id=1, source_target_pairs={{0,1},{1,0},{2,3},{3,2},{4,5},{5,4},{6,7},{7,6},{8,9},{9,8},{10,11... | collective-permute-start | bytes 786440 | tf_op jit(solution)/shard_map/ppermute | solution.py:379
  3.0 9.9 %collective-permute-start.1 = (bf16[256,512]{1,0:T(8,128)(2,1)}, bf16[256,512]{1,0:T(8,128)(2,1)S(1)}, u32[]{:S(2)}, u32[]{:S(2)}) collective-permute-start(bf16[256,512]{1,0:T(8,128)(2,1)} %refs_0_.1), channel_id=1, source_target_pairs={{0,2},{1,3},{2,4},{3,5},{4,6},{5,7},{6,0},{7,1},{8,10},{9,11},{10,... | collective-permute-start | bytes 786440 | tf_op jit(solution)/shard_map/ppermute | solution.py:379
  14.3 21.7 %collective-permute-start.8 = (bf16[256,512]{1,0:T(8,128)(2,1)S(1)}, bf16[256,512]{1,0:T(8,128)(2,1)S(1)}, u32[]{:S(2)}, u32[]{:S(2)}) collective-permute-start(bf16[256,512]{1,0:T(8,128)(2,1)S(1)} %copy-done.5), channel_id=1, source_target_pairs={{0,6},{1,7},{2,0},{3,1},{4,2},{5,3},{6,4},{7,5},{8,14},{9,15},{10,... | collective-permute-start | bytes 786440 | tf_op jit(solution)/shard_map/ppermute | solution.py:379
  18.4 9.1 %collective-permute-start.3 = (bf16[128,288]{1,0:T(8,128)(2,1)S(1)}, bf16[128,288]{1,0:T(8,128)(2,1)S(1)}, u32[]{:S(2)}, u32[]{:S(2)}) collective-permute-start(bf16[128,288]{1,0:T(8,128)(2,1)S(1)} %add_convert_fusion.13.refs_7_), channel_id=1, source_target_pairs={{0,2},{1,3},{2,0},{3,1},{4,6},{5,7},{6,4},{7,5},{8,10},{9,11},{10,... | collective-permute-start | bytes 221192 | tf_op jit(solution)/shard_map/ppermute | solution.py:383
  18.6 21.0 %collective-permute-start.10 = (bf16[256,512]{1,0:T(8,128)(2,1)S(1)}, bf16[256,512]{1,0:T(8,128)(2,1)S(1)}, u32[]{:S(2)}, u32[]{:S(2)}) collective-permute-start(bf16[256,512]{1,0:T(8,128)(2,1)S(1)} %collective-permute-done.1.refs_1_.refs_0_), channel_id=1, source_target_pairs={{0,1},{1,0},{2,3},{3,2},{4,5},{5,4},{6,7},{7,6},{8,9},{9,8},{10,11... | collective-permute-start | bytes 786440 | tf_op jit(solution)/shard_map/ppermute | solution.py:379
  19.2 19.0 %collective-permute-start.6 = (bf16[256,512]{1,0:T(8,128)(2,1)S(1)}, bf16[256,512]{1,0:T(8,128)(2,1)S(1)}, u32[]{:S(2)}, u32[]{:S(2)}) collective-permute-start(bf16[256,512]{1,0:T(8,128)(2,1)S(1)} %collective-permute-done.1.refs_1_.refs_0_), channel_id=1, source_target_pairs={{0,2},{1,3},{2,4},{3,5},{4,6},{5,7},{6,0},{7,1},{8,10},{9,11},{10,... | collective-permute-start | bytes 786440 | tf_op jit(solution)/shard_map/ppermute | solution.py:379
  27.5 9.9 %collective-permute-start.4 = (bf16[128,288]{1,0:T(8,128)(2,1)S(1)}, bf16[128,288]{1,0:T(8,128)(2,1)S(1)}, u32[]{:S(2)}, u32[]{:S(2)}) collective-permute-start(bf16[128,288]{1,0:T(8,128)(2,1)S(1)} %add_convert_fusion.12.refs_7_), channel_id=1, source_target_pairs={{0,4},{1,5},{2,6},{3,7},{4,0},{5,1},{6,2},{7,3},{8,12},{9,13},{10,... | collective-permute-start | bytes 221192 | tf_op jit(solution)/shard_map/ppermute | solution.py:383
  36.0 9.9 %collective-permute-start.9 = (bf16[256,512]{1,0:T(8,128)(2,1)S(1)}, bf16[256,512]{1,0:T(8,128)(2,1)S(1)}, u32[]{:S(2)}, u32[]{:S(2)}) collective-permute-start(bf16[256,512]{1,0:T(8,128)(2,1)S(1)} %collective-permute-done.8.refs_0_), channel_id=1, source_target_pairs={{0,1},{1,0},{2,3},{3,2},{4,5},{5,4},{6,7},{7,6},{8,9},{9,8},{10,11... | collective-permute-start | bytes 786440 | tf_op jit(solution)/shard_map/ppermute | solution.py:379
  37.5 14.5 %collective-permute-start.5 = (bf16[128,288]{1,0:T(8,128)(2,1)S(1)}, bf16[128,288]{1,0:T(8,128)(2,1)S(1)}, u32[]{:S(2)}, u32[]{:S(2)}) collective-permute-start(bf16[128,288]{1,0:T(8,128)(2,1)S(1)} %get-tuple-element.130.refs_7_), channel_id=1, source_target_pairs={{0,1},{1,0},{2,3},{3,2},{4,5},{5,4},{6,7},{7,6},{8,9},{9,8},{10,11... | collective-permute-start | bytes 221192 | tf_op jit(solution)/shard_map/ppermute | solution.py:379
  38.2 13.9 %collective-permute-start.7 = (bf16[256,512]{1,0:T(8,128)(2,1)S(1)}, bf16[256,512]{1,0:T(8,128)(2,1)S(1)}, u32[]{:S(2)}, u32[]{:S(2)}) collective-permute-start(bf16[256,512]{1,0:T(8,128)(2,1)S(1)} %collective-permute-done.6.refs_0_), channel_id=1, source_target_pairs={{0,1},{1,0},{2,3},{3,2},{4,5},{5,4},{6,7},{7,6},{8,9},{9,8},{10,11... | collective-permute-start | bytes 786440 | tf_op jit(solution)/shard_map/ppermute | solution.py:379
  82.5 13.2 %collective-permute-start.14 = (bf16[256,512]{1,0:T(8,128)(2,1)S(1)}, bf16[256,512]{1,0:T(8,128)(2,1)S(1)}, u32[]{:S(2)}, u32[]{:S(2)}) collective-permute-start(bf16[256,512]{1,0:T(8,128)(2,1)S(1)} %get-tuple-element.96), channel_id=1, source_target_pairs={{0,1},{1,0},{2,3},{3,2},{4,5},{5,4},{6,7},{7,6},{8,9},{9,8},{10,11... | collective-permute-start | bytes 786440 | tf_op jit(solution)/shard_map/ppermute | solution.py:379
  93.6 9.2 %collective-permute-start.13 = (bf16[256,512]{1,0:T(8,128)(2,1)S(1)}, bf16[256,512]{1,0:T(8,128)(2,1)S(1)}, u32[]{:S(2)}, u32[]{:S(2)}) collective-permute-start(bf16[256,512]{1,0:T(8,128)(2,1)S(1)} %get-tuple-element.93), channel_id=1, source_target_pairs={{0,1},{1,0},{2,3},{3,2},{4,5},{5,4},{6,7},{7,6},{8,9},{9,8},{10,11... | collective-permute-start | bytes 786440 | tf_op jit(solution)/shard_map/ppermute | solution.py:379
  95.1 15.7 %collective-permute-start.12 = (bf16[256,512]{1,0:T(8,128)(2,1)S(1)}, bf16[256,512]{1,0:T(8,128)(2,1)S(1)}, u32[]{:S(2)}, u32[]{:S(2)}) collective-permute-start(bf16[256,512]{1,0:T(8,128)(2,1)S(1)} %get-tuple-element.89), channel_id=1, source_target_pairs={{0,1},{1,0},{2,3},{3,2},{4,5},{5,4},{6,7},{7,6},{8,9},{9,8},{10,11... | collective-permute-start | bytes 786440 | tf_op jit(solution)/shard_map/ppermute | solution.py:379
  95.8 15.0 %collective-permute-start.15 = (bf16[256,512]{1,0:T(8,128)(2,1)S(1)}, bf16[256,512]{1,0:T(8,128)(2,1)S(1)}, u32[]{:S(2)}, u32[]{:S(2)}) collective-permute-start(bf16[256,512]{1,0:T(8,128)(2,1)S(1)} %add_convert_fusion.7), channel_id=1, source_target_pairs={{0,2},{1,3},{2,4},{3,5},{4,6},{5,7},{6,0},{7,1},{8,10},{9,11},{10,... | collective-permute-start | bytes 786440 | tf_op jit(solution)/shard_map/ppermute | solution.py:379
  96.5 19.1 %collective-permute-start.11 = (bf16[256,512]{1,0:T(8,128)(2,1)S(1)}, bf16[256,512]{1,0:T(8,128)(2,1)S(1)}, u32[]{:S(2)}, u32[]{:S(2)}) collective-permute-start(bf16[256,512]{1,0:T(8,128)(2,1)S(1)} %get-tuple-element.88), channel_id=1, source_target_pairs={{0,1},{1,0},{2,3},{3,2},{4,5},{5,4},{6,7},{7,6},{8,9},{9,8},{10,11... | collective-permute-start | bytes 786440 | tf_op jit(solution)/shard_map/ppermute | solution.py:379
  108.5 12.0 %collective-permute-start.17 = (bf16[256,512]{1,0:T(8,128)(2,1)S(1)}, bf16[256,512]{1,0:T(8,128)(2,1)S(1)}, u32[]{:S(2)}, u32[]{:S(2)}) collective-permute-start(bf16[256,512]{1,0:T(8,128)(2,1)S(1)} %add_convert_fusion.5), channel_id=1, source_target_pairs={{0,6},{1,7},{2,0},{3,1},{4,2},{5,3},{6,4},{7,5},{8,14},{9,15},{10,... | collective-permute-start | bytes 786440 | tf_op jit(solution)/shard_map/ppermute | solution.py:379
  111.5 11.6 %collective-permute-start.16 = (bf16[256,512]{1,0:T(8,128)(2,1)S(1)}, bf16[256,512]{1,0:T(8,128)(2,1)S(1)}, u32[]{:S(2)}, u32[]{:S(2)}) collective-permute-start(bf16[256,512]{1,0:T(8,128)(2,1)S(1)} %add_convert_fusion.6), channel_id=1, source_target_pairs={{0,2},{1,3},{2,4},{3,5},{4,6},{5,7},{6,0},{7,1},{8,10},{9,11},{10,... | collective-permute-start | bytes 786440 | tf_op jit(solution)/shard_map/ppermute | solution.py:379
  126.0 8.2 %collective-permute-start.19 = (bf16[256,512]{1,0:T(8,128)(2,1)S(1)}, bf16[256,512]{1,0:T(8,128)(2,1)S(1)}, u32[]{:S(2)}, u32[]{:S(2)}) collective-permute-start(bf16[256,512]{1,0:T(8,128)(2,1)S(1)} %add_convert_fusion.4.rows_ref.refs_0_), channel_id=1, source_target_pairs={{0,2},{1,3},{2,4},{3,5},{4,6},{5,7},{6,0},{7,1},{8,10},{9,11},{10,... | collective-permute-start | bytes 786440 | tf_op jit(solution)/shard_map/ppermute | solution.py:379
  139.8 6.8 %collective-permute-start.21 = (bf16[128,288]{1,0:T(8,128)(2,1)S(1)}, bf16[128,288]{1,0:T(8,128)(2,1)S(1)}, u32[]{:S(2)}, u32[]{:S(2)}) collective-permute-start(bf16[128,288]{1,0:T(8,128)(2,1)S(1)} %add_convert_fusion.10.refs_7_), channel_id=1, source_target_pairs={{0,2},{1,3},{2,0},{3,1},{4,6},{5,7},{6,4},{7,5},{8,10},{9,11},{10,... | collective-permute-start | bytes 221192 | tf_op jit(solution)/shard_map/ppermute | solution.py:383
  139.9 11.3 %collective-permute-start.26 = (bf16[256,512]{1,0:T(8,128)(2,1)S(1)}, bf16[256,512]{1,0:T(8,128)(2,1)S(1)}, u32[]{:S(2)}, u32[]{:S(2)}) collective-permute-start(bf16[256,512]{1,0:T(8,128)(2,1)S(1)} %add_convert_fusion.4.rows_ref.refs_0_), channel_id=1, source_target_pairs={{0,6},{1,7},{2,0},{3,1},{4,2},{5,3},{6,4},{7,5},{8,14},{9,15},{10,... | collective-permute-start | bytes 786440 | tf_op jit(solution)/shard_map/ppermute | solution.py:379
  141.9 16.8 %collective-permute-start.28 = (bf16[256,512]{1,0:T(8,128)(2,1)S(1)}, bf16[256,512]{1,0:T(8,128)(2,1)S(1)}, u32[]{:S(2)}, u32[]{:S(2)}) collective-permute-start(bf16[256,512]{1,0:T(8,128)(2,1)S(1)} %collective-permute-done.19.refs_1_.refs_0_), channel_id=1, source_target_pairs={{0,1},{1,0},{2,3},{3,2},{4,5},{5,4},{6,7},{7,6},{8,9},{9,8},{10,11... | collective-permute-start | bytes 786440 | tf_op jit(solution)/shard_map/ppermute | solution.py:379
  143.1 14.5 %collective-permute-start.24 = (bf16[256,512]{1,0:T(8,128)(2,1)S(1)}, bf16[256,512]{1,0:T(8,128)(2,1)S(1)}, u32[]{:S(2)}, u32[]{:S(2)}) collective-permute-start(bf16[256,512]{1,0:T(8,128)(2,1)S(1)} %collective-permute-done.19.refs_1_.refs_0_), channel_id=1, source_target_pairs={{0,2},{1,3},{2,4},{3,5},{4,6},{5,7},{6,0},{7,1},{8,10},{9,11},{10,... | collective-permute-start | bytes 786440 | tf_op jit(solution)/shard_map/ppermute | solution.py:379
  146.6 10.0 %collective-permute-start.22 = (bf16[128,288]{1,0:T(8,128)(2,1)S(1)}, bf16[128,288]{1,0:T(8,128)(2,1)S(1)}, u32[]{:S(2)}, u32[]{:S(2)}) collective-permute-start(bf16[128,288]{1,0:T(8,128)(2,1)S(1)} %add_convert_fusion.9.refs_7_), channel_id=1, source_target_pairs={{0,4},{1,5},{2,6},{3,7},{4,0},{5,1},{6,2},{7,3},{8,12},{9,13},{10,... | collective-permute-start | bytes 221192 | tf_op jit(solution)/shard_map/ppermute | solution.py:383
  151.2 9.4 %collective-permute-start.27 = (bf16[256,512]{1,0:T(8,128)(2,1)S(1)}, bf16[256,512]{1,0:T(8,128)(2,1)S(1)}, u32[]{:S(2)}, u32[]{:S(2)}) collective-permute-start(bf16[256,512]{1,0:T(8,128)(2,1)S(1)} %collective-permute-done.26.refs_0_), channel_id=1, source_target_pairs={{0,1},{1,0},{2,3},{3,2},{4,5},{5,4},{6,7},{7,6},{8,9},{9,8},{10,11... | collective-permute-start | bytes 786440 | tf_op jit(solution)/shard_map/ppermute | solution.py:379
  157.6 7.0 %collective-permute-start.25 = (bf16[256,512]{1,0:T(8,128)(2,1)S(1)}, bf16[256,512]{1,0:T(8,128)(2,1)S(1)}, u32[]{:S(2)}, u32[]{:S(2)}) collective-permute-start(bf16[256,512]{1,0:T(8,128)(2,1)S(1)} %collective-permute-done.24.refs_0_), channel_id=1, source_target_pairs={{0,1},{1,0},{2,3},{3,2},{4,5},{5,4},{6,7},{7,6},{8,9},{9,8},{10,11... | collective-permute-start | bytes 786440 | tf_op jit(solution)/shard_map/ppermute | solution.py:379
  194.7 13.9 %collective-permute-start.31 = (bf16[256,512]{1,0:T(8,128)(2,1)S(1)}, bf16[256,512]{1,0:T(8,128)(2,1)S(1)}, u32[]{:S(2)}, u32[]{:S(2)}) collective-permute-start(bf16[256,512]{1,0:T(8,128)(2,1)S(1)} %get-tuple-element.124), channel_id=1, source_target_pairs={{0,1},{1,0},{2,3},{3,2},{4,5},{5,4},{6,7},{7,6},{8,9},{9,8},{10,11... | collective-permute-start | bytes 786440 | tf_op jit(solution)/shard_map/ppermute | solution.py:379
  206.5 9.2 %collective-permute-start.34 = (bf16[256,512]{1,0:T(8,128)(2,1)S(1)}, bf16[256,512]{1,0:T(8,128)(2,1)S(1)}, u32[]{:S(2)}, u32[]{:S(2)}) collective-permute-start(bf16[256,512]{1,0:T(8,128)(2,1)S(1)} %get-tuple-element.126), channel_id=1, source_target_pairs={{0,1},{1,0},{2,3},{3,2},{4,5},{5,4},{6,7},{7,6},{8,9},{9,8},{10,11... | collective-permute-start | bytes 786440 | tf_op jit(solution)/shard_map/ppermute | solution.py:379
  207.3 14.1 %collective-permute-start.30 = (bf16[256,512]{1,0:T(8,128)(2,1)S(1)}, bf16[256,512]{1,0:T(8,128)(2,1)S(1)}, u32[]{:S(2)}, u32[]{:S(2)}) collective-permute-start(bf16[256,512]{1,0:T(8,128)(2,1)S(1)} %get-tuple-element.122), channel_id=1, source_target_pairs={{0,1},{1,0},{2,3},{3,2},{4,5},{5,4},{6,7},{7,6},{8,9},{9,8},{10,11... | collective-permute-start | bytes 786440 | tf_op jit(solution)/shard_map/ppermute | solution.py:379
  208.6 12.7 %collective-permute-start.32 = (bf16[256,512]{1,0:T(8,128)(2,1)S(1)}, bf16[256,512]{1,0:T(8,128)(2,1)S(1)}, u32[]{:S(2)}, u32[]{:S(2)}) collective-permute-start(bf16[256,512]{1,0:T(8,128)(2,1)S(1)} %add_convert_fusion.3), channel_id=1, source_target_pairs={{0,2},{1,3},{2,4},{3,5},{4,6},{5,7},{6,0},{7,1},{8,10},{9,11},{10,... | collective-permute-start | bytes 786440 | tf_op jit(solution)/shard_map/ppermute | solution.py:379
  210.0 16.0 %collective-permute-start.29 = (bf16[256,512]{1,0:T(8,128)(2,1)S(1)}, bf16[256,512]{1,0:T(8,128)(2,1)S(1)}, u32[]{:S(2)}, u32[]{:S(2)}) collective-permute-start(bf16[256,512]{1,0:T(8,128)(2,1)S(1)} %get-tuple-element.120), channel_id=1, source_target_pairs={{0,1},{1,0},{2,3},{3,2},{4,5},{5,4},{6,7},{7,6},{8,9},{9,8},{10,11... | collective-permute-start | bytes 786440 | tf_op jit(solution)/shard_map/ppermute | solution.py:379
  215.8 10.3 %collective-permute-start.35 = (bf16[256,512]{1,0:T(8,128)(2,1)S(1)}, bf16[256,512]{1,0:T(8,128)(2,1)S(1)}, u32[]{:S(2)}, u32[]{:S(2)}) collective-permute-start(bf16[256,512]{1,0:T(8,128)(2,1)S(1)} %add_convert_fusion.1), channel_id=1, source_target_pairs={{0,6},{1,7},{2,0},{3,1},{4,2},{5,3},{6,4},{7,5},{8,14},{9,15},{10,... | collective-permute-start | bytes 786440 | tf_op jit(solution)/shard_map/ppermute | solution.py:379
  221.4 8.4 %collective-permute-start.33 = (bf16[256,512]{1,0:T(8,128)(2,1)S(1)}, bf16[256,512]{1,0:T(8,128)(2,1)S(1)}, u32[]{:S(2)}, u32[]{:S(2)}) collective-permute-start(bf16[256,512]{1,0:T(8,128)(2,1)S(1)} %add_convert_fusion.2), channel_id=1, source_target_pairs={{0,2},{1,3},{2,4},{3,5},{4,6},{5,7},{6,0},{7,1},{8,10},{9,11},{10,... | collective-permute-start | bytes 786440 | tf_op jit(solution)/shard_map/ppermute | solution.py:379
  (18 other events, 121.6 us)
